TPU v7x, 128 devices: a whole 4x4x4 slice. The times are simulated.
128 devices in a mesh: leaf: 8 (over x, core), space: 16 (over y, z).
Axes of the slice: x: 4, y: 4, z: 4, core: 2. Of those that a mesh axis runs over, the one named last changes fastest.
Arguments:
- basis: bfloat16 [8, 262144, 256], P('leaf', 'space'), may hold values from -6 to 6
- sing_vals: float32 [8, 256], P('leaf'), may hold values from 0.7 to 1.4
- sketch: float32 [512, 256], replicated, may hold values from -6 to 6
Outputs:
- fresh: bfloat16 [8, 262144, 256], P('leaf', 'space')
- correlation: float32 [8, 256, 256], P('leaf')
All inputs are finite; a program needn't handle non-finite values.
Results may differ from a plain program's by a relative error of at most 0.012.
Values may be sent and summed in bfloat16 or wider, within the bound.
A program may use at most 128 MiB of HBM per device.

v0:
```python
import jax
import jax.numpy as jnp
from jax import lax
from jax.sharding import PartitionSpec as P

ITERS = 2


def from_partner(value, axis, stride):
    return lax.ppermute(value, axis, [(i, i ^ 1 << stride) for i in range(lax.axis_size(axis))])


def orthonormal(block):
    inner = jnp.dot(block.T, block, precision=lax.Precision.HIGHEST)
    lower = jnp.linalg.cholesky(inner)
    return lax.linalg.triangular_solve(lower, block, left_side=False, lower=True, transpose_a=True)


def on_device(basis, sing_vals, sketch):
    contract = (((0,), (0,)), ((), ()))
    points = basis.shape[1] * lax.axis_size("space")
    own = (basis[0].astype(jnp.float32) * sing_vals[0][None, :]).astype(jnp.bfloat16)
    other = from_partner(own, "leaf", 0)
    is_even = lax.axis_index("leaf") % 2 == 0
    even = jnp.where(is_even, own, other)
    odd = jnp.where(is_even, other, own)
    merged = jnp.concatenate([even, odd], axis=1)
    local_gram = lax.dot_general(merged, merged, contract, preferred_element_type=jnp.float32)
    gram = lax.psum(local_gram, "space")
    block = sketch
    for step in range(ITERS):
        block = orthonormal(jnp.dot(gram, block, precision=lax.Precision.HIGHEST))
    block_b = block.astype(jnp.bfloat16)
    weights = block_b.astype(jnp.float32)
    fresh = jnp.dot(merged, block_b, preferred_element_type=jnp.float32).astype(jnp.bfloat16)
    cross_terms = lax.dot_general(own, merged, contract, preferred_element_type=jnp.float32)
    local_term = jnp.dot(cross_terms, weights, precision=lax.Precision.HIGHEST)
    correlation = lax.psum(local_term.astype(jnp.bfloat16), "space").astype(jnp.float32) / points
    return (fresh[None], correlation[None])


def solution(mesh):
    in_specs = (P("leaf", "space", None), P("leaf", None), P())
    out_specs = (P("leaf", "space", None), P("leaf", None, None))
    return jax.shard_map(
        on_device, mesh=mesh, in_specs=in_specs, out_specs=out_specs, check_vma=False
    )
```

profile of v0, /device:TPU:1, one launch (start us, length us, event | category | flops | bytes accessed | tf_op | source)
XLA Modules:
  0.0 365.5 jit_solution(15470636422054899849)
XLA Ops:
  7.2 0.0 copy-start
  7.2 0.0 all-reduce.4.cloned.1.call-start
  7.2 0.0 copy-start.3
  7.2 7.7 %fusion.1 = bf16[16384,256]{1,0:T(8,128)(2,1)} fusion(bf16[1,16384,256]{2,1,0:T(8,128)(2,1)} %param.6, f32[256]{0:T(256)} %bitcast.86), kind=kLoop, calls=%fused_computation.8 | loop fusion | flops 12582912 | bytes 16778240 | tf_op jit(solution)/shard_map/convert_element_type | solution.py:22
  15.0 1.4 collective-permute-start
  16.4 13.1 %collective-permute-done = bf16[16384,256]{1,0:T(8,128)(2,1)} collective-permute-done((bf16[16384,256]{1,0:T(8,128)(2,1)}, bf16[16384,256]{1,0:T(8,128)(2,1)}, u32[]{:S(2)}, u32[]{:S(2)}) %collective-permute-start) | collective-permute-done | bytes 8388640 | tf_op jit(solution)/shard_map/ppermute | solution.py:10
  29.5 0.0 copy-done.3
  29.5 10.5 %broadcast_select_fusion.1 = (bf16[16384,256]{1,0:T(8,128)(2,1)S(1)}, bf16[16384,256]{1,0:T(8,128)(2,1)}) fusion(bf16[16384,256]{1,0:T(8,128)(2,1)} %collective-permute-done, pred[]{:T(512)S(6)} %eq.5, f32[256]{0:T(256)S(1)} %bitcast.87, bf16[1,16384,256]{2,1,0:T(8,128)(2,1)} %param.6), kind=kLoop, calls=%fused_computation.10 | loop fusion | flops 20971520 | bytes 33555456 | tf_op jit(solution)/shard_map/jit(_where)/select_n | solution.py:25
  40.0 0.0 copy-start.1
  40.0 3.2 copy-done.1
  43.2 14.5 %fusion.3 = f32[512,512]{1,0:T(8,128)} fusion(bf16[16384,256]{1,0:T(8,128)(2,1)} %get-tuple-element.41, bf16[16384,256]{1,0:T(8,128)(2,1)S(1)} %get-tuple-element.40), kind=kOutput, calls=%fused_computation.12 | convolution fusion | flops 8623489024 | bytes 17825792 | tf_op jit(solution)/shard_map/dot_general | solution.py:28
  57.7 0.0 all-reduce.4.cloned.1.call-update
  57.8 0.0 all-reduce.6.cloned.1.call-start
  57.8 13.1 %fusion.2 = f32[256,512]{1,0:T(8,128)S(1)} fusion(bf16[16384,256]{1,0:T(8,128)(2,1)} %fusion.1, bf16[16384,256]{1,0:T(8,128)(2,1)} %get-tuple-element.41, bf16[16384,256]{1,0:T(8,128)(2,1)} %copy-done.1), kind=kOutput, calls=%fused_computation.11 | convolution fusion | flops 4328521728 | bytes 25690112 | tf_op jit(solution)/shard_map/dot_general | solution.py:36
  70.9 74.8 %all-reduce.4.cloned.1.call-done = f32[512,512]{1,0:T(8,128)} async-done(((f32[512,512]{1,0:T(8,128)}), f32[512,512]{1,0:T(8,128)}) %all-reduce.4.cloned.1.call-update) | async-done | bytes 1048592 | tf_op jit(solution)/shard_map/psum | solution.py:29
  145.7 0.0 copy-done
  145.7 0.0 copy-start.2
  145.7 2.3 fusion.36
  148.0 1.0 fusion.37
  149.0 0.1 copy.5
  149.2 11.7 %cholesky.130 = f32[128,128]{1,0:T(8,128)S(1)} custom-call(f32[128,128]{1,0:T(8,128)S(1)} %cholesky.194), custom_call_target="Cholesky" | custom-call | tf_op jit(solution)/shard_map/jit(cholesky)/cholesky | solution.py:15
  161.0 9.8 %custom-call.13 = f32[1,128,128]{1,2,0:T(8,128)S(1)} custom-call(f32[1,128,128]{2,1,0:T(8,128)S(1)} %get-tuple-element.49), custom_call_target="InvertDiagBlocksLowerTriangular" | custom-call | tf_op jit(solution)/shard_map/jit(cholesky)/cholesky | solution.py:15
  170.8 0.2 constant_dynamic-update-slice_fusion.3
  171.0 0.3 convolution_subtract_fusion.3
  171.3 11.9 %cholesky.147 = f32[128,128]{1,0:T(8,128)S(1)} custom-call(f32[128,128]{1,0:T(8,128)S(1)} %convolution_subtract_fusion.3), custom_call_target="Cholesky" | custom-call | tf_op jit(solution)/shard_map/jit(cholesky)/cholesky | solution.py:15
  183.2 0.6 compare_reduce_fusion.2
  185.1 0.1 broadcast.91
  185.2 3.8 %while.4 = (s32[]{:T(128)}, f32[256,256]{1,0:T(8,128)S(1)}, s32[2,2]{1,0:T(2,128)S(1)}, f32[2,128,128]{2,1,0:T(8,128)S(1)}, s32[]{:T(128)}) while((s32[]{:T(128)}, f32[256,256]{1,0:T(8,128)S(1)}, s32[2,2]{1,0:T(2,128)S(1)}, f32[2,128,128]{2,1,0:T(8,128)S(1)}, s32[]{:T(128)}) %tuple.48), condition=%wide.while_cond, body=%wide.while_body.sunk | while | flops 2 | bytes 131181 | solution.py:16
  185.2 0.6 fusion.58
  185.8 1.3 bitcast_dynamic-update-slice_fusion.4
  187.1 0.6 fusion.58
  187.7 1.3 bitcast_dynamic-update-slice_fusion.4
  189.0 19.7 %custom-call.14 = f32[2,128,128]{1,2,0:T(8,128)S(1)} custom-call(f32[2,128,128]{2,1,0:T(8,128)S(1)} %get-tuple-element.18), custom_call_target="InvertDiagBlocksLowerTriangular" | custom-call | tf_op jit(solution)/shard_map/triangular_solve/custom-call.0 | solution.py:16
  208.7 0.4 fusion.10
  209.1 0.6 convolution_subtract_fusion.1
  209.7 0.4 fusion.18
  210.2 0.0 copy-done.2
  210.2 1.0 fusion.4
  211.2 1.0 fusion.38
  212.2 0.1 copy.6
  212.4 11.7 %cholesky.164 = f32[128,128]{1,0:T(8,128)S(1)} custom-call(f32[128,128]{1,0:T(8,128)S(1)} %cholesky.197), custom_call_target="Cholesky" | custom-call | tf_op jit(solution)/shard_map/jit(cholesky)/cholesky | solution.py:15
  224.2 9.8 %custom-call.15 = f32[1,128,128]{1,2,0:T(8,128)S(1)} custom-call(f32[1,128,128]{2,1,0:T(8,128)S(1)} %get-tuple-element.45), custom_call_target="InvertDiagBlocksLowerTriangular" | custom-call | tf_op jit(solution)/shard_map/jit(cholesky)/cholesky | solution.py:15
  234.0 0.2 constant_dynamic-update-slice_fusion.1
  234.2 0.3 convolution_subtract_fusion.2
  234.5 11.9 %cholesky.181 = f32[128,128]{1,0:T(8,128)S(1)} custom-call(f32[128,128]{1,0:T(8,128)S(1)} %convolution_subtract_fusion.2), custom_call_target="Cholesky" | custom-call | tf_op jit(solution)/shard_map/jit(cholesky)/cholesky | solution.py:15
  246.5 0.6 compare_reduce_fusion
  247.1 0.6 compare_reduce_fusion.1
  249.0 3.8 %while.5 = (s32[]{:T(128)}, f32[256,256]{1,0:T(8,128)S(1)}, s32[2,2]{1,0:T(2,128)S(1)}, f32[2,128,128]{2,1,0:T(8,128)S(1)}, s32[]{:T(128)}) while((s32[]{:T(128)}, f32[256,256]{1,0:T(8,128)S(1)}, s32[2,2]{1,0:T(2,128)S(1)}, f32[2,128,128]{2,1,0:T(8,128)S(1)}, s32[]{:T(128)}) %tuple.58), condition=%wide.while_cond.clone, body=%wide.while_body.clone.sunk | while | flops 2 | bytes 131181 | solution.py:16
  249.0 0.6 fusion.59
  249.6 1.3 bitcast_dynamic-update-slice_fusion.5
  251.0 0.6 fusion.59
  251.5 1.3 bitcast_dynamic-update-slice_fusion.5
  252.8 19.7 %custom-call.16 = f32[2,128,128]{1,2,0:T(8,128)S(1)} custom-call(f32[2,128,128]{2,1,0:T(8,128)S(1)} %get-tuple-element.19), custom_call_target="InvertDiagBlocksLowerTriangular" | custom-call | tf_op jit(solution)/shard_map/triangular_solve/custom-call.0 | solution.py:16
  272.5 0.4 fusion.8
  273.0 0.6 convolution_subtract_fusion
  273.6 0.4 fusion.14
  274.0 1.1 convolution_convert_fusion.1
  275.0 0.0 all-reduce.6.cloned.1.call-update
  275.1 10.3 %fusion = bf16[1,16384,256]{2,1,0:T(8,128)(2,1)} fusion(bf16[16384,256]{1,0:T(8,128)(2,1)} %get-tuple-element.41, bf16[16384,256]{1,0:T(8,128)(2,1)} %copy-done.1, bf16[512,128]{0,1:T(8,128)(2,1)S(1)} %fusion.14, f32[512,128]{0,1:T(8,128)S(1)} %bitcast.84), kind=kOutput, calls=%fused_computation.5 | convolution fusion | flops 4333240320 | bytes 25559040 | tf_op jit(solution)/shard_map/dot_general | solution.py:35
  285.3 71.3 %all-reduce.6.cloned.1.call-done = bf16[256,256]{1,0:T(8,128)(2,1)} async-done(((bf16[256,256]{1,0:T(8,128)(2,1)}), bf16[256,256]{1,0:T(8,128)(2,1)}) %all-reduce.6.cloned.1.call-update) | async-done | bytes 131088 | tf_op jit(solution)/shard_map/psum | solution.py:38
  356.6 1.6 multiply_bitcast_fusion
  (19 shorter events, 0.4 us)
Async XLA Ops:
  7.2 138.5 %copy-start = (f32[512,256]{1,0:T(8,128)S(1)}, f32[512,256]{1,0:T(8,128)}, u32[]{:S(2)}) copy-start(f32[512,256]{1,0:T(8,128)} %param.8) | copy-start | bytes 1572868
  7.2 138.5 %all-reduce.4.cloned.1.call-start = ((), (), s32[]{:S(2)}) async-start(), calls=%async_computation | async-start | bytes 2097152 | tf_op jit(solution)/shard_map/psum | solution.py:29
  7.2 22.3 %copy-start.3 = (f32[1,256]{1,0:T(1,128)S(1)}, f32[1,256]{1,0:T(1,128)}, u32[]{:S(2)}) copy-start(f32[1,256]{1,0:T(1,128)} %param.7) | copy-start | bytes 3076
  15.0 14.5 %collective-permute-start = (bf16[16384,256]{1,0:T(8,128)(2,1)}, bf16[16384,256]{1,0:T(8,128)(2,1)}, u32[]{:S(2)}, u32[]{:S(2)}) collective-permute-start(bf16[16384,256]{1,0:T(8,128)(2,1)} %fusion.1), channel_id=1, source_target_pairs={{0,16},{16,0},{32,48},{48,32},{64,80},{80,64},{96,112},{112,96},{1... | collective-permute-start | bytes 25165832 | tf_op jit(solution)/shard_map/ppermute | solution.py:10
  40.0 3.2 copy-start.1
  57.8 298.9 %all-reduce.6.cloned.1.call-start = ((), (), s32[]{:S(2)}) async-start(), calls=%async_computation.1 | async-start | bytes 262144 | tf_op jit(solution)/shard_map/psum | solution.py:38
  145.7 64.5 %copy-start.2 = (f32[512,512]{1,0:T(8,128)S(1)}, f32[512,512]{1,0:T(8,128)}, u32[]{:S(2)}) copy-start(f32[512,512]{1,0:T(8,128)} %all-reduce.4.cloned.1.call-done) | copy-start | bytes 3145732
Sparse Core Ops, SparseCore 0:
  57.9 87.7 all-reduce.3
  275.2 81.3 all-reduce.5
where the time goes:
time: 372 us; the launch traced here: 366 us
  waiting for transfers between devices  159 us (43%)
  other arithmetic  128 us (34%)
  matrix products  48.1 us (13%)
  between operations  17.2 us (5%)
  local copies, waits for them, and re-layouts  11.2 us (3%)
    psum x1, waiting for transfers between devices, on_device(): gram = lax.psum(local_gram, 'space')  74.8 us
    psum x1, waiting for transfers between devices, on_device(): lax.psum(local_term.astype(jnp.bfloat16), 'space').astype(jnp.float32)  71.3 us
    another operation x13, other arithmetic, orthonormal(): lower = jnp.linalg.cholesky(inner)  68.9 us
    another operation x5, other arithmetic, orthonormal(): lax.linalg.triangular_solve(lower, block, left_side=False, lower=True, tr...  39.4 us
    dot_general x1, matrix products, on_device(): lax.dot_general(merged, merged, contract, preferred_element_type=jnp.floa...  14.5 us
    ppermute x1, waiting for transfers between devices, from_partner(): lax.ppermute(value, axis, [(i, i ^ 1 << stride) for i in range(lax.axis_s...  13.1 us
    dot_general x1, matrix products, on_device(): lax.dot_general(own, merged, contract, preferred_element_type=jnp.float32)  13.1 us
    select_n x1, other arithmetic, on_device(): even = jnp.where(is_even, own, other)  10.5 us
  transfers between devices with their start and end apart: 3, of which 3 were waited for; matrix products, arithmetic and copies ran while one was open for 6% of the time, Pallas kernels for 0%

commit v1 on v0

--- a/solution.py
+++ b/solution.py
@@ -33,9 +33,8 @@
     block_b = block.astype(jnp.bfloat16)
     weights = block_b.astype(jnp.float32)
     fresh = jnp.dot(merged, block_b, preferred_element_type=jnp.float32).astype(jnp.bfloat16)
-    cross_terms = lax.dot_general(own, merged, contract, preferred_element_type=jnp.float32)
-    local_term = jnp.dot(cross_terms, weights, precision=lax.Precision.HIGHEST)
-    correlation = lax.psum(local_term.astype(jnp.bfloat16), "space").astype(jnp.float32) / points
+    own_rows = lax.dynamic_slice_in_dim(gram, (lax.axis_index("leaf") % 2) * own.shape[1], own.shape[1], 0)
+    correlation = jnp.dot(own_rows, weights, precision=lax.Precision.HIGHEST) / points
     return (fresh[None], correlation[None])
 
 

time: 372 us -> 307 us (0.83)
  waiting for transfers between devices: 159 us -> 101 us
  matrix products: 48.1 us -> 35.3 us
  other arithmetic: 128 us -> 137 us
    psum x1 -> x0, waiting for transfers between devices: 71.3 us -> none  [on_device(): lax.psum(local_term.astype(jnp.bfloat16), 'space').astype(jnp.float32)]
    psum x1, waiting for transfers between devices: 74.8 us -> 87.9 us  [on_device(): gram = lax.psum(local_gram, 'space')]
    dot_general x2 -> x1, matrix products: 14.2 us -> 1.12 us  [on_device(): jnp.dot(own_rows, weights, precision=lax.Precision.HIGHEST) / points]
    another operation x13, other arithmetic: 68.9 us -> 79 us  [orthonormal(): lower = jnp.linalg.cholesky(inner)]
  transfers between devices with their start and end apart: 3 -> 2, of which waited for: 3 -> 2; matrix products, arithmetic and copies ran while one was open for 6% -> 0% of each run, Pallas kernels for 0% -> 0%
where the time goes in v1:
time: 307 us; the launch traced here: 304 us
  other arithmetic  137 us (45%)
  waiting for transfers between devices  101 us (33%)
  matrix products  35.3 us (11%)
  between operations  17.2 us (6%)
  local copies, waits for them, and re-layouts  11.6 us (4%)
    psum x1, waiting for transfers between devices, on_device(): gram = lax.psum(local_gram, 'space')  87.9 us
    another operation x13, other arithmetic, orthonormal(): lower = jnp.linalg.cholesky(inner)  79 us
    another operation x5, other arithmetic, orthonormal(): lax.linalg.triangular_solve(lower, block, left_side=False, lower=True, tr...  39.4 us
    dot_general x1, matrix products, on_device(): lax.dot_general(merged, merged, contract, preferred_element_type=jnp.floa...  14.8 us
    ppermute x1, waiting for transfers between devices, from_partner(): lax.ppermute(value, axis, [(i, i ^ 1 << stride) for i in range(lax.axis_s...  13.1 us
    select_n x1, other arithmetic, on_device(): even = jnp.where(is_even, own, other)  10.5 us
    dot_general x1, matrix products, on_device(): jnp.dot(merged, block_b, preferred_element_type=jnp.float32)  10.3 us
    another operation x15, local copies, waits for them, and re-layouts, orthonormal(): lax.linalg.triangular_solve(lower, block, left_side=False, lower=True, tr...  8.09 us
  transfers between devices with their start and end apart: 2, of which 2 were waited for; matrix products, arithmetic and copies ran while one was open for 0% of the time, Pallas kernels for 0%

profile of v1, /device:TPU:1, one launch (start us, length us, event | category | flops | bytes accessed | tf_op | source)
XLA Modules:
  0.0 303.5 jit_solution(12696520379351341154)
XLA Ops:
  7.2 0.0 copy-start
  7.2 0.0 all-reduce.3.cloned.1.call-start
  7.2 0.0 copy-start.3
  7.2 7.8 %fusion.1 = bf16[16384,256]{1,0:T(8,128)(2,1)} fusion(bf16[1,16384,256]{2,1,0:T(8,128)(2,1)} %param.6, f32[256]{0:T(256)} %bitcast.84), kind=kLoop, calls=%fused_computation.8 | loop fusion | flops 12582912 | bytes 16778240 | tf_op jit(solution)/shard_map/convert_element_type | solution.py:22
  15.0 1.4 collective-permute-start
  16.4 13.1 %collective-permute-done = bf16[16384,256]{1,0:T(8,128)(2,1)} collective-permute-done((bf16[16384,256]{1,0:T(8,128)(2,1)}, bf16[16384,256]{1,0:T(8,128)(2,1)}, u32[]{:S(2)}, u32[]{:S(2)}) %collective-permute-start) | collective-permute-done | bytes 8388640 | tf_op jit(solution)/shard_map/ppermute | solution.py:10
  29.6 0.0 copy-done.3
  29.6 10.5 %broadcast_select_fusion.1 = (bf16[16384,256]{1,0:T(8,128)(2,1)S(1)}, bf16[16384,256]{1,0:T(8,128)(2,1)}) fusion(bf16[16384,256]{1,0:T(8,128)(2,1)} %collective-permute-done, pred[]{:T(512)S(6)} %eq.6, f32[256]{0:T(256)S(1)} %bitcast.85, bf16[1,16384,256]{2,1,0:T(8,128)(2,1)} %param.6), kind=kLoop, calls=%fused_computation.11 | loop fusion | flops 20971520 | bytes 33555456 | tf_op jit(solution)/shard_map/jit(_where)/select_n | solution.py:25
  40.1 0.0 copy-start.1
  40.1 3.2 %copy-done.1 = bf16[16384,256]{1,0:T(8,128)(2,1)} copy-done((bf16[16384,256]{1,0:T(8,128)(2,1)}, bf16[16384,256]{1,0:T(8,128)(2,1)S(1)}, u32[]{:S(2)}) %copy-start.1) | copy-done | bytes 8388632
  43.3 14.8 %fusion.2 = f32[512,512]{1,0:T(8,128)} fusion(bf16[16384,256]{1,0:T(8,128)(2,1)} %get-tuple-element.41, bf16[16384,256]{1,0:T(8,128)(2,1)S(1)} %get-tuple-element.40), kind=kOutput, calls=%fused_computation.9 | convolution fusion | flops 8623489024 | bytes 17825792 | tf_op jit(solution)/shard_map/dot_general | solution.py:28
  58.1 0.0 all-reduce.3.cloned.1.call-update
  58.1 87.9 %all-reduce.3.cloned.1.call-done = f32[512,512]{1,0:T(8,128)} async-done(((f32[512,512]{1,0:T(8,128)}), f32[512,512]{1,0:T(8,128)}) %all-reduce.3.cloned.1.call-update) | async-done | bytes 1048592 | tf_op jit(solution)/shard_map/psum | solution.py:29
  146.0 0.0 copy-done
  146.0 0.0 copy-start.2
  146.0 2.3 fusion.37
  148.3 1.0 fusion.38
  149.4 0.1 copy.5
  149.6 11.7 %cholesky.130 = f32[128,128]{1,0:T(8,128)S(1)} custom-call(f32[128,128]{1,0:T(8,128)S(1)} %cholesky.194), custom_call_target="Cholesky" | custom-call | tf_op jit(solution)/shard_map/jit(cholesky)/cholesky | solution.py:15
  161.3 9.8 %custom-call.13 = f32[1,128,128]{1,2,0:T(8,128)S(1)} custom-call(f32[1,128,128]{2,1,0:T(8,128)S(1)} %get-tuple-element.49), custom_call_target="InvertDiagBlocksLowerTriangular" | custom-call | tf_op jit(solution)/shard_map/jit(cholesky)/cholesky | solution.py:15
  171.1 0.2 constant_dynamic-update-slice_fusion.3
  171.4 0.3 convolution_subtract_fusion.3
  171.6 21.9 %cholesky.147 = f32[128,128]{1,0:T(8,128)S(1)} custom-call(f32[128,128]{1,0:T(8,128)S(1)} %convolution_subtract_fusion.3), custom_call_target="Cholesky" | custom-call | tf_op jit(solution)/shard_map/jit(cholesky)/cholesky | solution.py:15
  193.6 0.7 compare_reduce_fusion.2
  195.7 0.1 broadcast.91
  195.8 4.1 %while.4 = (s32[]{:T(128)}, f32[256,256]{1,0:T(8,128)S(1)}, s32[2,2]{1,0:T(2,128)S(1)}, f32[2,128,128]{2,1,0:T(8,128)S(1)}, s32[]{:T(128)}) while((s32[]{:T(128)}, f32[256,256]{1,0:T(8,128)S(1)}, s32[2,2]{1,0:T(2,128)S(1)}, f32[2,128,128]{2,1,0:T(8,128)S(1)}, s32[]{:T(128)}) %tuple.48), condition=%wide.while_cond, body=%wide.while_body.sunk | while | flops 2 | bytes 131181 | solution.py:16
  195.8 0.6 fusion.57
  196.4 1.4 bitcast_dynamic-update-slice_fusion.4
  197.9 0.6 fusion.57
  198.5 1.4 bitcast_dynamic-update-slice_fusion.4
  199.9 19.7 %custom-call.14 = f32[2,128,128]{1,2,0:T(8,128)S(1)} custom-call(f32[2,128,128]{2,1,0:T(8,128)S(1)} %get-tuple-element.18), custom_call_target="InvertDiagBlocksLowerTriangular" | custom-call | tf_op jit(solution)/shard_map/triangular_solve/custom-call.0 | solution.py:16
  219.6 0.4 fusion.11
  220.0 0.6 convolution_subtract_fusion.1
  220.6 0.4 fusion.19
  221.0 0.0 copy-done.2
  221.0 1.0 fusion.4
  222.1 1.0 fusion.39
  223.1 0.1 copy.6
  223.3 11.7 %cholesky.164 = f32[128,128]{1,0:T(8,128)S(1)} custom-call(f32[128,128]{1,0:T(8,128)S(1)} %cholesky.197), custom_call_target="Cholesky" | custom-call | tf_op jit(solution)/shard_map/jit(cholesky)/cholesky | solution.py:15
  235.1 9.8 %custom-call.15 = f32[1,128,128]{1,2,0:T(8,128)S(1)} custom-call(f32[1,128,128]{2,1,0:T(8,128)S(1)} %get-tuple-element.45), custom_call_target="InvertDiagBlocksLowerTriangular" | custom-call | tf_op jit(solution)/shard_map/jit(cholesky)/cholesky | solution.py:15
  244.9 0.2 constant_dynamic-update-slice_fusion.1
  245.1 0.3 convolution_subtract_fusion.2
  245.4 11.9 %cholesky.181 = f32[128,128]{1,0:T(8,128)S(1)} custom-call(f32[128,128]{1,0:T(8,128)S(1)} %convolution_subtract_fusion.2), custom_call_target="Cholesky" | custom-call | tf_op jit(solution)/shard_map/jit(cholesky)/cholesky | solution.py:15
  257.3 0.6 compare_reduce_fusion
  257.9 0.6 compare_reduce_fusion.1
  259.9 4.0 %while.5 = (s32[]{:T(128)}, f32[256,256]{1,0:T(8,128)S(1)}, s32[2,2]{1,0:T(2,128)S(1)}, f32[2,128,128]{2,1,0:T(8,128)S(1)}, s32[]{:T(128)}) while((s32[]{:T(128)}, f32[256,256]{1,0:T(8,128)S(1)}, s32[2,2]{1,0:T(2,128)S(1)}, f32[2,128,128]{2,1,0:T(8,128)S(1)}, s32[]{:T(128)}) %tuple.56), condition=%wide.while_cond.clone, body=%wide.while_body.clone.sunk | while | flops 2 | bytes 131181 | solution.py:16
  259.9 0.6 fusion.58
  260.5 1.4 bitcast_dynamic-update-slice_fusion.5
  261.9 0.6 fusion.58
  262.5 1.4 bitcast_dynamic-update-slice_fusion.5
  263.9 19.7 %custom-call.16 = f32[2,128,128]{1,2,0:T(8,128)S(1)} custom-call(f32[2,128,128]{2,1,0:T(8,128)S(1)} %get-tuple-element.19), custom_call_target="InvertDiagBlocksLowerTriangular" | custom-call | tf_op jit(solution)/shard_map/triangular_solve/custom-call.0 | solution.py:16
  283.6 0.4 fusion.9
  284.0 0.6 convolution_subtract_fusion
  284.6 0.4 fusion.15
  285.0 10.3 %fusion = bf16[1,16384,256]{2,1,0:T(8,128)(2,1)} fusion(bf16[16384,256]{1,0:T(8,128)(2,1)} %get-tuple-element.41, bf16[16384,256]{1,0:T(8,128)(2,1)} %copy-done.1, bf16[512,128]{0,1:T(8,128)(2,1)S(1)} %fusion.15, f32[512,128]{0,1:T(8,128)S(1)} %bitcast.81), kind=kOutput, calls=%fused_computation.5 | convolution fusion | flops 4333240320 | bytes 25559040 | tf_op jit(solution)/shard_map/dot_general | solution.py:35
  295.3 1.1 fusion.3
  (19 shorter events, 0.4 us)
Async XLA Ops:
  7.2 138.9 %copy-start = (f32[512,256]{1,0:T(8,128)S(1)}, f32[512,256]{1,0:T(8,128)}, u32[]{:S(2)}) copy-start(f32[512,256]{1,0:T(8,128)} %param.8) | copy-start | bytes 1572868
  7.2 138.8 %all-reduce.3.cloned.1.call-start = ((), (), s32[]{:S(2)}) async-start(), calls=%async_computation | async-start | bytes 2097152 | tf_op jit(solution)/shard_map/psum | solution.py:29
  7.2 22.4 %copy-start.3 = (f32[1,256]{1,0:T(1,128)S(1)}, f32[1,256]{1,0:T(1,128)}, u32[]{:S(2)}) copy-start(f32[1,256]{1,0:T(1,128)} %param.7) | copy-start | bytes 3076
  15.0 14.5 %collective-permute-start = (bf16[16384,256]{1,0:T(8,128)(2,1)}, bf16[16384,256]{1,0:T(8,128)(2,1)}, u32[]{:S(2)}, u32[]{:S(2)}) collective-permute-start(bf16[16384,256]{1,0:T(8,128)(2,1)} %fusion.1), channel_id=1, source_target_pairs={{0,16},{16,0},{32,48},{48,32},{64,80},{80,64},{96,112},{112,96},{1... | collective-permute-start | bytes 25165832 | tf_op jit(solution)/shard_map/ppermute | solution.py:10
  40.1 3.2 %copy-start.1 = (bf16[16384,256]{1,0:T(8,128)(2,1)}, bf16[16384,256]{1,0:T(8,128)(2,1)S(1)}, u32[]{:S(2)}) copy-start(bf16[16384,256]{1,0:T(8,128)(2,1)S(1)} %get-tuple-element.40) | copy-start | bytes 25165828
  146.0 75.0 %copy-start.2 = (f32[512,512]{1,0:T(8,128)S(1)}, f32[512,512]{1,0:T(8,128)}, u32[]{:S(2)}) copy-start(f32[512,512]{1,0:T(8,128)} %all-reduce.3.cloned.1.call-done) | copy-start | bytes 3145732
Sparse Core Ops, SparseCore 0:
  58.2 87.7 all-reduce.2

commit v2 on v1

v2 whole, which is shorter than its diff:
```python
import functools
import jax
import jax.numpy as jnp
from jax import lax
from jax.experimental import pallas as pl
from jax.experimental.pallas import tpu as pltpu
from jax.sharding import PartitionSpec as P

ITERS = 2
PANEL = 32
SUB = 16
EXACT = lax.Precision.HIGHEST


def dot(a, b, on_a, on_b, precision=EXACT):
    dims = (((on_a,), (on_b,)), ((), ()))
    return lax.dot_general(a, b, dims, precision=precision, preferred_element_type=jnp.float32)


def inverse_factor(inner):
    n = inner.shape[0]
    count = n // PANEL
    wide = n // 128
    lane = lax.broadcasted_iota(jnp.int32, (PANEL, n), 1)
    row = lax.broadcasted_iota(jnp.int32, (PANEL, 128), 0)
    row_wide = lax.broadcasted_iota(jnp.int32, (PANEL, n), 0)
    panels = [inner[i * PANEL : (i + 1) * PANEL] for i in range(count)]
    done = []
    for p in range(count):
        w = panels[p]
        first = p * PANEL
        diag = jnp.zeros((PANEL, 128), jnp.float32)
        for sub in range(0, PANEL, SUB):
            cols = [
                jnp.broadcast_to(w[:, first + sub + j : first + sub + j + 1], (PANEL, 128))
                for j in range(SUB)
            ]
            for j in range(SUB):
                at = sub + j
                top = at // 8 * 8
                inv = (1.0 / jnp.broadcast_to(cols[j][at : at + 1], (8, 128)))[0:1]
                mult = jnp.where(row[top:] > at, cols[j][top:] * inv, 0.0)
                for k in range(j + 1, SUB):
                    low = cols[k][top:] - mult * cols[k][at : at + 1]
                    cols[k] = jnp.concatenate([cols[k][:top], low], axis=0) if top else low
                diag = jnp.where(row == at, cols[j], diag)
                unit = jnp.where(row_wide[top:] == at, 1.0, 0.0)
                low = jnp.where(lane[top:] == first + at, unit, w[top:])
                low = low - jnp.concatenate([mult] * wide, axis=1) * low[at - top : at - top + 1]
                if top:
                    low = jnp.concatenate(
                        [jnp.where(lane[:top] == first + at, 0.0, w[:top]), low], axis=0
                    )
                w = low
        w = w * jnp.concatenate([lax.rsqrt(diag)] * wide, axis=1)
        done.append(jnp.where(lane < first + PANEL, w, 0.0) if p + 1 < count else w)
        blank = (lane >= first) & (lane < first + PANEL)
        if p + 1 < count:
            after = first + PANEL
            near = dot(w[:, after : after + PANEL], w, 0, 0)
            panels[p + 1] = jnp.where(blank, 0.0, panels[p + 1]) - near
        if p + 2 < count:
            far = dot(w[:, after + PANEL :], w, 0, 0)
            for m in range(p + 2, count):
                at = (m - p - 2) * PANEL
                panels[m] = jnp.where(blank, 0.0, panels[m]) - far[at : at + PANEL]
    return jnp.concatenate(done, axis=0)


def subspace_kernel(points, gram_ref, sketch_ref, own_ref, q_ref, corr_ref):
    gram = gram_ref[...]
    block = sketch_ref[...].T
    for _ in range(ITERS):
        y = dot(block, gram, 1, 0)
        block = dot(inverse_factor(dot(y, y, 1, 1)), y, 1, 0)
    q_b = block.T.astype(jnp.bfloat16)
    q_ref[...] = q_b
    corr_ref[...] = dot(own_ref[...], q_b.astype(jnp.float32), 1, 0) * (1.0 / points)


def from_partner(value, axis, stride):
    return lax.ppermute(value, axis, [(i, i ^ 1 << stride) for i in range(lax.axis_size(axis))])


def on_device(basis, sing_vals, sketch):
    contract = (((0,), (0,)), ((), ()))
    points = basis.shape[1] * lax.axis_size("space")
    own = (basis[0].astype(jnp.float32) * sing_vals[0][None, :]).astype(jnp.bfloat16)
    other = from_partner(own, "leaf", 0)
    is_even = lax.axis_index("leaf") % 2 == 0
    even = jnp.where(is_even, own, other)
    odd = jnp.where(is_even, other, own)
    merged = jnp.concatenate([even, odd], axis=1)
    local_gram = lax.dot_general(merged, merged, contract, preferred_element_type=jnp.float32)
    gram = lax.psum(local_gram, "space")
    kept = own.shape[1]
    own_rows = lax.dynamic_slice_in_dim(gram, (lax.axis_index("leaf") % 2) * kept, kept, 0)
    block_b, correlation = pl.pallas_call(
        functools.partial(subspace_kernel, points),
        out_shape=(
            jax.ShapeDtypeStruct(sketch.shape, jnp.bfloat16),
            jax.ShapeDtypeStruct((kept, kept), jnp.float32),
        ),
        compiler_params=pltpu.CompilerParams(vmem_limit_bytes=32 * 1024 * 1024),
        name="subspace",
    )(gram, sketch, own_rows)
    fresh = jnp.dot(merged, block_b, preferred_element_type=jnp.float32).astype(jnp.bfloat16)
    return (fresh[None], correlation[None])


def solution(mesh):
    in_specs = (P("leaf", "space", None), P("leaf", None), P())
    out_specs = (P("leaf", "space", None), P("leaf", None, None))
    return jax.shard_map(
        on_device, mesh=mesh, in_specs=in_specs, out_specs=out_specs, check_vma=False
    )
```

time: 307 us -> 190 us (0.62)
  other arithmetic: 137 us -> 20.3 us
  Pallas kernels: 0 us -> 20.9 us
  local copies, waits for them, and re-layouts: 11.6 us -> 2.3 us
  matrix products: 35.3 us -> 29.1 us
  between operations: 17.2 us -> 14.1 us
    another operation x18 -> x0, other arithmetic: 118 us -> none  [the longest x13 79 us: orthonormal(): lower = jnp.linalg.cholesky(inner)]
    pallas_call x0 -> x1, Pallas kernels: none -> 20.9 us  [on_device(): pl.pallas_call(functools.partial(subspace_kernel, points), out_shape=(jax...]
    another operation x19 -> x0, local copies, waits for them, and re-layouts: 8.14 us -> none  [the longest x15 8.09 us: orthonormal(): lax.linalg.triangular_solve(lower, block, left_side=False, lower=True, tr...]
    dot_general x5 -> x0, matrix products: 6.48 us -> none  [the longest x2 3.32 us: on_device(): block = orthonormal(jnp.dot(gram, block, precision=lax.Precision.HIGHEST))]
    dot_general x1, matrix products: 14.8 us -> 18.8 us  [on_device(): lax.dot_general(merged, merged, contract, preferred_element_type=jnp.floa...]
    another operation x10 -> x0, matrix products: 3.79 us -> none  [the longest x6 2.85 us: orthonormal(): lax.linalg.triangular_solve(lower, block, left_side=False, lower=True, tr...]
where the time goes in v2:
time: 190 us; the launch traced here: 189 us
  waiting for transfers between devices  101 us (53%)
  matrix products  29.1 us (15%)
  Pallas kernels  20.9 us (11%)
  other arithmetic  20.3 us (11%)
  between operations  14.1 us (7%)
  local copies, waits for them, and re-layouts  2.3 us (1%)
    psum x1, waiting for transfers between devices, on_device(): gram = lax.psum(local_gram, 'space')  88 us
    pallas_call x1, Pallas kernels, on_device(): pl.pallas_call(functools.partial(subspace_kernel, points), out_shape=(jax...  20.9 us
    dot_general x1, matrix products, on_device(): lax.dot_general(merged, merged, contract, preferred_element_type=jnp.floa...  18.8 us
    ppermute x1, waiting for transfers between devices, from_partner(): lax.ppermute(value, axis, [(i, i ^ 1 << stride) for i in range(lax.axis_s...  13.1 us
    select_n x1, other arithmetic, on_device(): even = jnp.where(is_even, own, other)  12.6 us
    dot_general x1, matrix products, on_device(): jnp.dot(merged, block_b, preferred_element_type=jnp.float32)  10.2 us
    convert_element_type x1, other arithmetic, on_device(): (basis[0].astype(jnp.float32) * sing_vals[0][None, :]).astype(jnp.bfloat16)  7.71 us
  transfers between devices with their start and end apart: 2, of which 2 were waited for; matrix products, arithmetic and copies ran while one was open for 0% of the time, Pallas kernels for 0%

profile of v2, /device:TPU:1, one launch (start us, length us, event | category | flops | bytes accessed | tf_op | source)
XLA Modules:
  0.0 189.3 jit_solution(11326762969185176694)
XLA Ops:
  7.2 0.0 all-reduce.2.cloned.1.call-start
  7.2 0.0 copy-start.2
  7.2 7.7 %fusion.1 = bf16[16384,256]{1,0:T(8,128)(2,1)} fusion(bf16[1,16384,256]{2,1,0:T(8,128)(2,1)} %param.3, f32[256]{0:T(256)} %bitcast.10), kind=kLoop, calls=%fused_computation.4 | loop fusion | flops 12582912 | bytes 16778240 | tf_op jit(solution)/shard_map/convert_element_type | solution.py:88
  14.9 1.4 collective-permute-start
  16.4 13.1 %collective-permute-done = bf16[16384,256]{1,0:T(8,128)(2,1)} collective-permute-done((bf16[16384,256]{1,0:T(8,128)(2,1)}, bf16[16384,256]{1,0:T(8,128)(2,1)}, u32[]{:S(2)}, u32[]{:S(2)}) %collective-permute-start) | collective-permute-done | bytes 8388640 | tf_op jit(solution)/shard_map/ppermute | solution.py:82
  29.5 0.0 copy-done.2
  29.5 12.6 %broadcast_select_fusion.1 = (bf16[16384,256]{1,0:T(8,128)(2,1)}, bf16[16384,256]{1,0:T(8,128)(2,1)}) fusion(bf16[16384,256]{1,0:T(8,128)(2,1)} %collective-permute-done, pred[]{:T(512)S(6)} %eq.6, f32[256]{0:T(256)S(1)} %bitcast.11, bf16[1,16384,256]{2,1,0:T(8,128)(2,1)} %param.3), kind=kLoop, calls=%fused_computation.7 | loop fusion | flops 20971520 | bytes 33555456 | tf_op jit(solution)/shard_map/jit(_where)/select_n | solution.py:91
  42.1 0.0 copy-start.1
  42.1 18.8 %fusion.2 = f32[512,512]{1,0:T(8,128)} fusion(bf16[16384,256]{1,0:T(8,128)(2,1)} %get-tuple-element.7, bf16[16384,256]{1,0:T(8,128)(2,1)} %get-tuple-element.6), kind=kOutput, calls=%fused_computation.5 | convolution fusion | flops 8623489024 | bytes 17825792 | tf_op jit(solution)/shard_map/dot_general | solution.py:94
  60.9 0.0 all-reduce.2.cloned.1.call-update
  61.0 88.0 %all-reduce.2.cloned.1.call-done.gram_ref = f32[512,512]{1,0:T(8,128)} async-done(((f32[512,512]{1,0:T(8,128)}), f32[512,512]{1,0:T(8,128)}) %all-reduce.2.cloned.1.call-update) | async-done | bytes 1048592 | tf_op jit(solution)/shard_map/psum | solution.py:95
  149.0 1.1 constant_dynamic-slice_fusion.own_ref
  150.1 0.0 copy-done.1
  150.1 0.0 copy-start
  150.1 1.2 copy-done
  151.3 20.9 %subspace.1 = (bf16[512,256]{1,0:T(8,128)(2,1)S(1)}, f32[256,256]{1,0:T(8,128)}) custom-call(f32[512,512]{1,0:T(8,128)S(1)} %copy-done, f32[512,256]{1,0:T(8,128)S(1)} %copy-done.1, f32[256,512]{1,0:T(8,128)S(1)} %constant_dynamic-slice_fusion.own_ref), custom_call_target="tpu_custom_call" | custom-call | tf_op jit(solution)/shard_map/subspace/pallas_call | solution.py:98
  172.2 10.2 %fusion = bf16[1,16384,256]{2,1,0:T(8,128)(2,1)} fusion(bf16[512,256]{1,0:T(8,128)(2,1)S(1)} %get-tuple-element.4, bf16[16384,256]{1,0:T(8,128)(2,1)} %get-tuple-element.7, bf16[16384,256]{1,0:T(8,128)(2,1)} %get-tuple-element.6), kind=kOutput, calls=%fused_computation.1 | convolution fusion | flops 4332716032 | bytes 25427968 | tf_op jit(solution)/shard_map/dot_general | solution.py:107
Async XLA Ops:
  7.2 141.8 %all-reduce.2.cloned.1.call-start = ((), (), s32[]{:S(2)}) async-start(), calls=%async_computation | async-start | bytes 2097152 | tf_op jit(solution)/shard_map/psum | solution.py:95
  7.2 22.3 %copy-start.2 = (f32[1,256]{1,0:T(1,128)S(1)}, f32[1,256]{1,0:T(1,128)}, u32[]{:S(2)}) copy-start(f32[1,256]{1,0:T(1,128)} %param.4) | copy-start | bytes 3076
  14.9 14.5 %collective-permute-start = (bf16[16384,256]{1,0:T(8,128)(2,1)}, bf16[16384,256]{1,0:T(8,128)(2,1)}, u32[]{:S(2)}, u32[]{:S(2)}) collective-permute-start(bf16[16384,256]{1,0:T(8,128)(2,1)} %fusion.1), channel_id=1, source_target_pairs={{0,16},{16,0},{32,48},{48,32},{64,80},{80,64},{96,112},{112,96},{1... | collective-permute-start | bytes 25165832 | tf_op jit(solution)/shard_map/ppermute | solution.py:82
  42.1 108.0 %copy-start.1 = (f32[512,256]{1,0:T(8,128)S(1)}, f32[512,256]{1,0:T(8,128)}, u32[]{:S(2)}) copy-start(f32[512,256]{1,0:T(8,128)} %sketch_ref.1) | copy-start | bytes 1572868
  150.1 1.2 copy-start
Sparse Core Ops, SparseCore 0:
  61.1 87.8 all-reduce.1

commit v3 on v2

--- a/solution.py
+++ b/solution.py
@@ -9,6 +9,9 @@
 ITERS = 2
 PANEL = 32
 SUB = 16
+CHUNK = 2048
+TILE = 2048
+MESH = pl.DeviceIdType.MESH
 EXACT = lax.Precision.HIGHEST
 
 
@@ -67,15 +70,188 @@
     return jnp.concatenate(done, axis=0)
 
 
-def subspace_kernel(points, gram_ref, sketch_ref, own_ref, q_ref, corr_ref):
-    gram = gram_ref[...]
+def exchange_kernel(
+    basis_ref, sing_ref, own_a, own_b, other_a, diag_ref, cross_ref,
+    turned, acc, acc_x, out_own, in_own, out_x, in_x,
+    load_sem, swap_send, swap_recv, send_sems, recv_sems,
+):
+    leaf, space = lax.axis_index("leaf"), lax.axis_index("space")
+    spaces = lax.axis_size("space")
+    peers = 2 * spaces
+    core, pair = lax.rem(leaf, 2), lax.div(leaf, 2)
+    me = space * 2 + core
+    partner = (leaf + 1 - 2 * core, space)
+    half = own_a.shape[0]
+    chunks = half // CHUNK
+
+    def peer(d):
+        to = lax.rem(me + d, peers)
+        return lax.rem(to, 2), lax.div(to, 2)
+
+    def load(part, start, i):
+        rows = pl.ds(pl.multiple_of(i * CHUNK, CHUNK), CHUNK)
+        source = pl.ds(pl.multiple_of(start + i * CHUNK, CHUNK), CHUNK)
+        return part.at[rows], basis_ref.at[0, source]
+
+    first, second = (1 - core) * half, core * half
+    for i in range(chunks):
+        to, source = load(own_a, first, i)
+        pltpu.make_async_copy(source, to, load_sem.at[i]).start()
+    for i in range(chunks):
+        to, source = load(own_b, second, i)
+        pltpu.make_async_copy(source, to, load_sem.at[chunks + i]).start()
+
+    barrier = pltpu.get_barrier_semaphore()
+
+    @pl.loop(1, peers)
+    def _(d):
+        to_core, to_space = peer(d)
+        pl.semaphore_signal(
+            barrier, inc=1, device_id=(pair * 2 + to_core, to_space), device_id_type=MESH
+        )
+
+    acc[...] = jnp.zeros_like(acc)
+    acc_x[...] = jnp.zeros_like(acc_x)
+    scale = sing_ref[...]
+
+    def scaled(part, i, start, sem):
+        to, source = load(part, start, i)
+        pltpu.make_async_copy(source, to, sem).wait()
+        rows = pl.ds(pl.multiple_of(i * CHUNK, CHUNK), CHUNK)
+        part[rows, :] = (part[rows, :].astype(jnp.float32) * scale).astype(jnp.bfloat16)
+        return rows
+
+    def swap(i):
+        rows = pl.ds(pl.multiple_of(i * CHUNK, CHUNK), CHUNK)
+        return pltpu.make_async_remote_copy(
+            src_ref=own_a.at[rows], dst_ref=other_a.at[rows], send_sem=swap_send.at[i],
+            recv_sem=swap_recv.at[i], device_id=partner, device_id_type=MESH,
+        )
+
+    def send(src, dst, which, to_core, to_space):
+        pltpu.make_async_remote_copy(
+            src_ref=src, dst_ref=dst, send_sem=send_sems.at[which], recv_sem=recv_sems.at[which],
+            device_id=(pair * 2 + to_core, to_space), device_id_type=MESH,
+        ).start()
+
+    def landed(ref, sem):
+        pltpu.make_async_copy(ref, ref, sem).wait()
+
+    scaled(own_a, 0, first, load_sem.at[0])
+    pl.semaphore_wait(barrier, peers - 1)
+    swap(0).start()
+
+    @pl.loop(1, chunks)
+    def _(i):
+        scaled(own_a, i, first, load_sem.at[i])
+        swap(i).start()
+
+    @pl.loop(0, chunks)
+    def _(i):
+        rows = pl.ds(pl.multiple_of(i * CHUNK, CHUNK), CHUNK)
+        value = own_a[rows, :]
+        acc[...] += dot(value, value, 0, 0, None)
+
+    @pl.loop(0, chunks)
+    def _(i):
+        rows = scaled(own_b, i, second, load_sem.at[chunks + i])
+        value = own_b[rows, :]
+        flipped = value.T
+        turned[i] = flipped
+        acc[...] += dot(flipped, value, 1, 0, None)
+
+    out_own[...] = acc[...].astype(out_own.dtype).reshape(out_own.shape)
+
+    @pl.loop(1, spaces)
+    def _(d):
+        to = lax.rem(space + d, spaces)
+        send(out_own.at[to], in_own.at[d - 1], 0, core, to)
+
+    @pl.loop(0, chunks)
+    def _(i):
+        swap(i).wait_recv()
+        rows = pl.ds(pl.multiple_of(i * CHUNK, CHUNK), CHUNK)
+        acc_x[...] += dot(turned[i], other_a[rows, :], 1, 0, None)
+
+    cross = acc_x[...]
+    cross = jnp.where(core == 0, cross, cross.T).astype(out_x.dtype)
+    wide = cross.shape[1] // 2
+    out_x[0] = cross[:, :wide].reshape(out_x.shape[1:])
+    out_x[1] = cross[:, wide:].reshape(out_x.shape[1:])
+
+    @pl.loop(1, peers)
+    def _(d):
+        to_core, to_space = peer(d)
+        send(out_x.at[to_core, to_space], in_x.at[d - 1], 1, to_core, to_space)
+
+    landed(in_own, recv_sems.at[0])
+    mine = acc[pl.ds(pl.multiple_of(space * 16, 16), 16), :]
+    diag_ref[me] = mine + jnp.sum(in_own[...].astype(jnp.float32), axis=0)
+
+    @pl.loop(1, peers)
+    def _(d):
+        to_core, to_space = peer(d)
+        send(diag_ref.at[me], diag_ref.at[me], 2, to_core, to_space)
+
+    landed(in_x, recv_sems.at[1])
+    mine = out_x[core, space].astype(jnp.float32)
+    cross_ref[me] = mine + jnp.sum(in_x[...].astype(jnp.float32), axis=0)
+
+    @pl.loop(1, peers)
+    def _(d):
+        to_core, to_space = peer(d)
+        send(cross_ref.at[me], cross_ref.at[me], 3, to_core, to_space)
+
+    landed(diag_ref.at[pl.ds(0, peers - 1)], recv_sems.at[2])
+    landed(cross_ref.at[pl.ds(0, peers - 1)], recv_sems.at[3])
+    landed(in_own, send_sems.at[0])
+    landed(in_x, send_sems.at[1])
+    landed(diag_ref.at[pl.ds(0, peers - 1)], send_sems.at[2])
+    landed(cross_ref.at[pl.ds(0, peers - 1)], send_sems.at[3])
+
+    @pl.loop(0, chunks)
+    def _(i):
+        swap(i).wait_send()
+
+
+def subspace_kernel(points, diag_ref, cross_ref, sketch_ref, q_ref, corr_ref, gram):
+    k = corr_ref.shape[0]
+    diag = diag_ref[...].reshape(k // 16, 2, 16, k)
+    cross = cross_ref[...].reshape(k // 16, 2, 16, k // 2)
+    corner = jnp.concatenate([cross[:, c].reshape(k, k // 2) for c in range(2)], axis=1)
+    gram[:k, :k] = diag[:, 0].reshape(k, k)
+    gram[k:, k:] = diag[:, 1].reshape(k, k)
+    gram[:k, k:] = corner
+    gram[k:, :k] = corner.T
     block = sketch_ref[...].T
     for _ in range(ITERS):
-        y = dot(block, gram, 1, 0)
+        y = dot(block, gram[...], 1, 0)
         block = dot(inverse_factor(dot(y, y, 1, 1)), y, 1, 0)
     q_b = block.T.astype(jnp.bfloat16)
     q_ref[...] = q_b
-    corr_ref[...] = dot(own_ref[...], q_b.astype(jnp.float32), 1, 0) * (1.0 / points)
+    own = pl.multiple_of(lax.rem(lax.axis_index("leaf"), 2) * k, k)
+    corr_ref[...] = dot(gram[pl.ds(own, k), :], q_b.astype(jnp.float32), 1, 0) * (1.0 / points)
+
+
+def fresh_kernel(own_a, own_b, other_a, other_b, q_ref, fresh_ref, held, sem):
+    core = lax.rem(lax.axis_index("leaf"), 2)
+    half, k = own_a.shape
+    own = pl.ds(pl.multiple_of(core * k, k), k)
+    rest = pl.ds(pl.multiple_of((1 - core) * k, k), k)
+    weights = jnp.concatenate([q_ref[own, :], q_ref[rest, :]], axis=0)
+    copies = []
+    for part, (mine, other) in enumerate(((own_a, other_b), (own_b, other_a))):
+        start = (1 - core if part == 0 else core) * half
+        for i in range(half // TILE):
+            rows = pl.ds(i * TILE, TILE)
+            at = pl.ds(part * half + i * TILE, TILE)
+            merged = jnp.concatenate([mine[rows, :], other[rows, :]], axis=1)
+            held[at, :] = dot(merged, weights, 1, 0, None).astype(jnp.bfloat16)
+            to = fresh_ref.at[0, pl.ds(pl.multiple_of(start + i * TILE, TILE), TILE)]
+            copies.append(pltpu.make_async_copy(held.at[at], to, sem.at[len(copies)]))
+            copies[-1].start()
+    for copy in copies:
+        copy.wait()
 
 
 def from_partner(value, axis, stride):
@@ -83,29 +259,71 @@
 
 
 def on_device(basis, sing_vals, sketch):
-    contract = (((0,), (0,)), ((), ()))
-    points = basis.shape[1] * lax.axis_size("space")
-    own = (basis[0].astype(jnp.float32) * sing_vals[0][None, :]).astype(jnp.bfloat16)
-    other = from_partner(own, "leaf", 0)
-    is_even = lax.axis_index("leaf") % 2 == 0
-    even = jnp.where(is_even, own, other)
-    odd = jnp.where(is_even, other, own)
-    merged = jnp.concatenate([even, odd], axis=1)
-    local_gram = lax.dot_general(merged, merged, contract, preferred_element_type=jnp.float32)
-    gram = lax.psum(local_gram, "space")
-    kept = own.shape[1]
-    own_rows = lax.dynamic_slice_in_dim(gram, (lax.axis_index("leaf") % 2) * kept, kept, 0)
+    rows, k = basis.shape[1:]
+    spaces = lax.axis_size("space")
+    points = rows * spaces
+    half = rows // 2
+    vmem = pl.BlockSpec(memory_space=pltpu.VMEM)
+    any_space = pl.BlockSpec(memory_space=pl.ANY)
+    f32, wire = jnp.float32, jnp.bfloat16
+    chunks = half // CHUNK
+    own_a, own_b, other_a, diag, cross = pl.pallas_call(
+        exchange_kernel,
+        out_shape=(
+            pltpu.VMEM((half, k), jnp.bfloat16),
+            pltpu.VMEM((half, k), jnp.bfloat16),
+            pltpu.VMEM((half, k), jnp.bfloat16),
+            pltpu.VMEM((2 * spaces, k // spaces, k), f32),
+            pltpu.VMEM((2 * spaces, k // spaces, k // 2), f32),
+        ),
+        in_specs=[pl.BlockSpec(memory_space=pltpu.HBM), vmem],
+        out_specs=(vmem,) * 5,
+        scratch_shapes=[
+            pltpu.VMEM((chunks, k, CHUNK), jnp.bfloat16),
+            pltpu.VMEM((k, k), f32),
+            pltpu.VMEM((k, k), f32),
+            pltpu.VMEM((spaces, k // spaces, k), wire),
+            pltpu.VMEM((spaces - 1, k // spaces, k), wire),
+            pltpu.VMEM((2, spaces, k // spaces, k // 2), wire),
+            pltpu.VMEM((2 * spaces - 1, k // spaces, k // 2), wire),
+            pltpu.SemaphoreType.DMA((2 * chunks,)),
+            pltpu.SemaphoreType.DMA((chunks,)),
+            pltpu.SemaphoreType.DMA((chunks,)),
+            pltpu.SemaphoreType.DMA((4,)),
+            pltpu.SemaphoreType.DMA((4,)),
+        ],
+        compiler_params=pltpu.CompilerParams(
+            collective_id=0, has_side_effects=True, vmem_limit_bytes=36 * 2**20
+        ),
+        name="exchange",
+    )(basis, sing_vals)
+    other_b = from_partner(own_b, "leaf", 0)
     block_b, correlation = pl.pallas_call(
         functools.partial(subspace_kernel, points),
         out_shape=(
             jax.ShapeDtypeStruct(sketch.shape, jnp.bfloat16),
-            jax.ShapeDtypeStruct((kept, kept), jnp.float32),
+            jax.ShapeDtypeStruct((k, k), f32),
         ),
-        compiler_params=pltpu.CompilerParams(vmem_limit_bytes=32 * 1024 * 1024),
+        in_specs=[vmem, vmem, vmem],
+        out_specs=(vmem, vmem),
+        scratch_shapes=[pltpu.VMEM((2 * k, 2 * k), f32)],
+        compiler_params=pltpu.CompilerParams(vmem_limit_bytes=16 * 2**20),
+        cost_estimate=pl.CostEstimate(flops=2**31, bytes_accessed=80 * 2**20, transcendentals=0),
         name="subspace",
-    )(gram, sketch, own_rows)
-    fresh = jnp.dot(merged, block_b, preferred_element_type=jnp.float32).astype(jnp.bfloat16)
-    return (fresh[None], correlation[None])
+    )(diag, cross, sketch)
+    fresh = pl.pallas_call(
+        fresh_kernel,
+        out_shape=jax.ShapeDtypeStruct((1, rows, k), jnp.bfloat16),
+        in_specs=[vmem] * 5,
+        out_specs=any_space,
+        scratch_shapes=[
+            pltpu.VMEM((rows, k), jnp.bfloat16),
+            pltpu.SemaphoreType.DMA((rows // TILE,)),
+        ],
+        compiler_params=pltpu.CompilerParams(vmem_limit_bytes=32 * 2**20),
+        name="fresh",
+    )(own_a, own_b, other_a, other_b, block_b)
+    return (fresh, correlation[None])
 
 
 def solution(mesh):

time: 190 us -> 58.4 us (0.31)
  waiting for transfers between devices: 101 us -> 0.01 us
  Pallas kernels: 20.9 us -> 56.3 us
  matrix products: 29.1 us -> 0 us
  other arithmetic: 20.3 us -> 0 us
  between operations: 14.1 us -> 0.81 us
    psum x1 -> x0, waiting for transfers between devices: 88 us -> none  [on_device(): gram = lax.psum(local_gram, 'space')]
    pallas_call x0 -> x2, Pallas kernels: none -> 35.5 us  [the longest x1 29.2 us: on_device(): pl.pallas_call(exchange_kernel, out_shape=(pltpu.VMEM((half, k), jnp.bflo...]
    dot_general x2 -> x0, matrix products: 29.1 us -> none  [the longest x1 18.8 us: on_device(): lax.dot_general(merged, merged, contract, preferred_element_type=jnp.floa...]
    ppermute x1, waiting for transfers between devices: 13.1 us -> 0.01 us  [from_partner(): lax.ppermute(value, axis, [(i, i ^ 1 << stride) for i in range(lax.axis_s...]
    select_n x1 -> x0, other arithmetic: 12.6 us -> none  [on_device(): even = jnp.where(is_even, own, other)]
    convert_element_type x1 -> x0, other arithmetic: 7.71 us -> none  [on_device(): (basis[0].astype(jnp.float32) * sing_vals[0][None, :]).astype(jnp.bfloat16)]
  transfers between devices with their start and end apart: 2 -> 1, of which waited for: 2 -> 0; matrix products, arithmetic and copies ran while one was open for 0% -> 0% of each run, Pallas kernels for 0% -> 36%
where the time goes in v3:
time: 58.4 us; the launch traced here: 58.3 us
  Pallas kernels  56.3 us (96%)
  between operations  0.81 us (1%)
  local copies, waits for them, and re-layouts  0.68 us (1%)
    pallas_call x1, Pallas kernels, on_device(): pl.pallas_call(exchange_kernel, out_shape=(pltpu.VMEM((half, k), jnp.bflo...  29.2 us
    pallas_call x1, Pallas kernels, on_device(): pl.pallas_call(functools.partial(subspace_kernel, points), out_shape=(jax...  20.8 us
    pallas_call x1, Pallas kernels, on_device(): pl.pallas_call(fresh_kernel, out_shape=jax.ShapeDtypeStruct((1, rows, k),...  6.26 us
  transfers between devices with their start and end apart: 1, of which 0 were waited for; matrix products, arithmetic and copies ran while one was open for 0% of the time, Pallas kernels for 36%

profile of v3, /device:TPU:1, one launch (start us, length us, event | category | flops | bytes accessed | tf_op | source)
XLA Modules:
  0.0 58.3 jit_solution(1367673045119652735)
XLA Ops:
  0.6 0.0 copy-start
  0.6 0.7 %copy-done = f32[1,256]{1,0:T(1,128)S(1)} copy-done((f32[1,256]{1,0:T(1,128)S(1)}, f32[1,256]{1,0:T(1,128)}, u32[]{:S(2)}) %copy-start) | copy-done | bytes 1048
  1.3 0.0 copy-start.1
  1.3 29.2 %exchange.1 = (bf16[8192,256]{1,0:T(8,128)(2,1)S(1)}, bf16[8192,256]{1,0:T(8,128)(2,1)S(1)}, bf16[8192,256]{1,0:T(8,128)(2,1)S(1)}, f32[32,16,256]{2,1,0:T(8,128)S(1)}, f32[32,16,128]{2,1,0:T(8,128)S(1)}) custom-call(bf16[1,16384,256]{2,1,0:T(8,128)(2,1)} %basis_ref.1, f32[1,256]{1,0:T(1,128)S(1)} %copy-done), custom_call_target="tpu_custom_call" | custom-call | tf_op jit(solution)/shard_map/exchange/pallas_call | solution.py:270
  30.6 0.5 collective-permute-start
  31.0 0.0 copy-done.1
  31.0 20.8 %subspace.1 = (bf16[512,256]{1,0:T(8,128)(2,1)S(1)}, f32[256,256]{1,0:T(8,128)}) custom-call(f32[32,16,256]{2,1,0:T(8,128)S(1)} %get-tuple-element.12.diag_ref, f32[32,16,128]{2,1,0:T(8,128)S(1)} %get-tuple-element.13.cross_ref, f32[512,256]{1,0:T(8,128)S(1)} %copy-done.1), custom_call_target="tpu_custom_call" | custom-call | flops 2147483648 | bytes 83886080 | tf_op jit(solution)/shard_map/subspace/pallas_call | solution.py:301
  51.9 0.0 collective-permute-done.other_b
  51.9 6.3 %fresh.1 = bf16[1,16384,256]{2,1,0:T(8,128)(2,1)} custom-call(bf16[8192,256]{1,0:T(8,128)(2,1)S(1)} %get-tuple-element.9.own_a, bf16[8192,256]{1,0:T(8,128)(2,1)S(1)} %get-tuple-element.10.own_b, bf16[8192,256]{1,0:T(8,128)(2,1)S(1)} %get-tuple-element.11.other_a, bf16[8192,256]{1,0:T(8,128)(2,1)S(1)} %collective-permute-done.other_b, ...), custom_call_target="tpu_custom_call" | custom-call | tf_op jit(solution)/shard_map/fresh/pallas_call | solution.py:314
Async XLA Ops:
  0.6 0.7 %copy-start = (f32[1,256]{1,0:T(1,128)S(1)}, f32[1,256]{1,0:T(1,128)}, u32[]{:S(2)}) copy-start(f32[1,256]{1,0:T(1,128)} %sing_ref.1) | copy-start | bytes 3076
  1.3 29.7 %copy-start.1 = (f32[512,256]{1,0:T(8,128)S(1)}, f32[512,256]{1,0:T(8,128)}, u32[]{:S(2)}) copy-start(f32[512,256]{1,0:T(8,128)} %sketch_ref.1) | copy-start | bytes 1572868
  30.6 21.3 %collective-permute-start = (bf16[8192,256]{1,0:T(8,128)(2,1)S(1)}, bf16[8192,256]{1,0:T(8,128)(2,1)S(1)}, u32[]{:S(2)}, u32[]{:S(2)}) collective-permute-start(bf16[8192,256]{1,0:T(8,128)(2,1)S(1)} %get-tuple-element.10.own_b), channel_id=1, source_target_pairs={{0,16},{16,0},{32,48},{48,32},{64,80},{80,64},{96,112},{112,96},{1... | collective-permute-start | bytes 12582920 | tf_op jit(solution)/shard_map/ppermute | solution.py:258

commit v4 on v3

v4 whole, which is shorter than its diff:
```python
import functools
import jax
import jax.numpy as jnp
from jax import lax
from jax.experimental import pallas as pl
from jax.experimental.pallas import tpu as pltpu
from jax.sharding import PartitionSpec as P

ITERS = 2
PANEL = 32
SUB = 16
CHUNK = 1024
STRIP = 2048
TILE = 2048
MESH = pl.DeviceIdType.MESH
EXACT = lax.Precision.HIGH


def dot(a, b, on_a, on_b, precision=EXACT):
    dims = (((on_a,), (on_b,)), ((), ()))
    return lax.dot_general(a, b, dims, precision=precision, preferred_element_type=jnp.float32)


def stack(block):
    terms = []
    for _ in range(3):
        terms.append(block.astype(jnp.bfloat16))
        block = block - terms[-1].astype(jnp.float32)
    high, mid, low = terms
    left = jnp.concatenate([high, mid, high, mid, low, high], axis=0)
    return left, jnp.concatenate([high, high, mid, mid, high, low], axis=0)


def inverse_factor(inner):
    n = inner.shape[0]
    count = n // PANEL
    tile = (8, 128)
    tall, wide = PANEL // 8, n // 128
    lane = lax.broadcasted_iota(jnp.int32, tile, 1)
    row = lax.broadcasted_iota(jnp.int32, tile, 0)
    lane_wide = lax.broadcasted_iota(jnp.int32, (PANEL, n), 1)
    unit = [jnp.where(row == s, 1.0, 0.0) for s in range(8)]
    panels = [inner[i * PANEL : (i + 1) * PANEL] for i in range(count)]
    done = []
    for p in range(count):
        first = p * PANEL
        here, base = first // 128, first % 128
        w = [
            [panels[p][8 * r : 8 * r + 8, 128 * h : 128 * h + 128] for h in range(wide)]
            for r in range(tall)
        ]
        diag = [jnp.zeros(tile, jnp.float32)] * tall
        for sub in range(0, PANEL, SUB):
            cols = [
                {
                    r: jnp.broadcast_to(w[r][here][:, base + sub + j : base + sub + j + 1], tile)
                    for r in range(sub // 8, tall)
                }
                for j in range(SUB)
            ]
            for j in range(SUB):
                at = sub + j
                top, s = at // 8, at % 8
                inv = 1.0 / jnp.broadcast_to(cols[j][top][s : s + 1], tile)
                mult = {r: cols[j][r] * inv for r in range(top, tall)}
                mult[top] = jnp.where(row > s, mult[top], 0.0)
                if s == 7:
                    del mult[top]
                for k in range(j + 1, SUB):
                    pivot = cols[k][top][s : s + 1]
                    for r in mult:
                        cols[k][r] = cols[k][r] - mult[r] * pivot
                diag[top] = jnp.where(row == s, cols[j][top], diag[top])
                at_lane = lane == base + at
                w[top][here] = jnp.where(at_lane, unit[s], w[top][here])
                for r in range(top + 1, tall):
                    w[r][here] = jnp.where(at_lane, 0.0, w[r][here])
                for h in range(wide):
                    pivot = w[top][h][s : s + 1]
                    for r in mult:
                        w[r][h] = w[r][h] - mult[r] * pivot
        for r in range(tall):
            scale = lax.rsqrt(diag[r])
            w[r] = [value * scale for value in w[r]]
            if r + 1 < tall:
                above = (lane >= base + 8 * r + 8) & (lane < base + PANEL)
                w[r][here] = jnp.where(above, 0.0, w[r][here])
        block = jnp.concatenate([jnp.concatenate(tiles, axis=1) for tiles in w], axis=0)
        after = first + PANEL
        if after == n:
            done.append(block)
            break
        done.append(jnp.where(lane_wide < after, block, 0.0))
        blank = (lane_wide >= first) & (lane_wide < after)
        left, right = stack(block)
        near = dot(left[:, after : after + PANEL], right, 0, 0, None)
        panels[p + 1] = jnp.where(blank, 0.0, panels[p + 1]) - near
        if after + PANEL < n:
            far = dot(left[:, after + PANEL :], right, 0, 0, None)
            for m in range(p + 2, count):
                at = (m - p - 2) * PANEL
                panels[m] = jnp.where(blank, 0.0, panels[m]) - far[at : at + PANEL]
    return jnp.concatenate(done, axis=0)


def exchange_kernel(
    basis_ref, sing_ref, own_a, own_b, other_a, diag_ref, cross_ref,
    sing, turned, acc, acc_x, out_own, in_own, out_x, in_x,
    answer, entered, sing_sem, load_sem, swap_send, swap_recv, send_sems, recv_sems,
):
    leaf, space = lax.axis_index("leaf"), lax.axis_index("space")
    spaces = lax.axis_size("space")
    peers = 2 * spaces
    core, pair = lax.rem(leaf, 2), lax.div(leaf, 2)
    me = space * 2 + core
    partner = (leaf + 1 - 2 * core, space)
    half = own_a.shape[0]
    chunks, strips = half // CHUNK, half // STRIP

    def away(i):
        side = 4
        k, m = lax.div(i, side), lax.rem(i, side)
        dy = lax.rem(2 + k + lax.div(k, 2) * (5 - 2 * k), side)
        dz = lax.rem(2 + m + lax.div(m, 2) * (5 - 2 * m), side)
        y, z = lax.div(space, side), lax.rem(space, side)
        return lax.rem(y + dy, side) * side + lax.rem(z + dz, side)

    def span(i, size, start=0):
        return pl.ds(pl.multiple_of(start + i * size, size), size)

    def load(part, start, i, size, sem):
        return pltpu.make_async_copy(
            basis_ref.at[0, span(i, size, start)], part.at[span(i, size)], sem
        )

    def scale(part, i, size):
        rows = span(i, size)
        part[rows, :] = (part[rows, :].astype(jnp.float32) * sing[...]).astype(jnp.bfloat16)

    def swap(i):
        return pltpu.make_async_remote_copy(
            src_ref=own_a.at[span(i, CHUNK)], dst_ref=other_a.at[span(i, CHUNK)],
            send_sem=swap_send.at[i], recv_sem=swap_recv.at[i],
            device_id=partner, device_id_type=MESH,
        )

    def send(src, dst, which, to_core, to_space):
        pltpu.make_async_remote_copy(
            src_ref=src, dst_ref=dst, send_sem=send_sems.at[which], recv_sem=recv_sems.at[which],
            device_id=(pair * 2 + to_core, to_space), device_id_type=MESH,
        ).start()

    def landed(ref, sem):
        pltpu.make_async_copy(ref, ref, sem).wait()

    sing_copy = pltpu.make_async_copy(sing_ref, sing, sing_sem)
    sing_copy.start()
    first, second = (1 - core) * half, core * half
    for i in range(chunks):
        load(own_a, first, i, CHUNK, load_sem.at[i]).start()
    for i in range(strips):
        load(own_b, second, i, STRIP, load_sem.at[chunks + i]).start()

    barrier = pltpu.get_barrier_semaphore()

    @pl.when(core == 1)
    def _():
        pl.semaphore_signal(barrier, inc=1, device_id=partner, device_id_type=MESH)

    @pl.when(core == 0)
    def _():
        pl.semaphore_wait(barrier, 1)
        pl.semaphore_signal(answer, inc=1, device_id=partner, device_id_type=MESH)

    @pl.when(core == 1)
    def _():
        pl.semaphore_wait(answer, 1)

        @pl.loop(0, spaces - 1)
        def _(i):
            pl.semaphore_signal(
                barrier, inc=1, device_id=(leaf, away(i)), device_id_type=MESH
            )

    acc[...] = jnp.zeros_like(acc)
    acc_x[...] = jnp.zeros_like(acc_x)
    sing_copy.wait()
    load(own_a, first, 0, CHUNK, load_sem.at[0]).wait()
    scale(own_a, 0, CHUNK)
    swap(0).start()

    @pl.loop(1, chunks)
    def _(i):
        load(own_a, first, i, CHUNK, load_sem.at[i]).wait()
        scale(own_a, i, CHUNK)
        swap(i).start()

    @pl.loop(0, strips)
    def _(i):
        value = own_a[span(i, STRIP), :]
        acc[...] += dot(value, value, 0, 0, None)

    @pl.loop(0, strips)
    def _(i):
        load(own_b, second, i, STRIP, load_sem.at[chunks + i]).wait()
        scale(own_b, i, STRIP)
        value = own_b[span(i, STRIP), :]
        flipped = value.T
        for part in range(STRIP // CHUNK):
            turned[i * (STRIP // CHUNK) + part] = flipped[:, part * CHUNK : (part + 1) * CHUNK]
        acc[...] += dot(flipped, value, 1, 0, None)

    @pl.when(core == 1)
    def _():
        pl.semaphore_wait(barrier, spaces - 1)
        pl.semaphore_signal(entered, inc=1, device_id=partner, device_id_type=MESH)

    @pl.when(core == 0)
    def _():
        pl.semaphore_wait(entered, 1)

    out_own[...] = acc[...].astype(out_own.dtype).reshape(out_own.shape)

    @pl.loop(0, spaces - 1)
    def _(i):
        to = away(i)
        send(out_own.at[to], in_own.at[i], 0, core, to)

    def add_cross(i):
        swap(i).wait_recv()
        acc_x[...] += dot(turned[i], other_a[span(i, CHUNK), :], 1, 0, None)

    @pl.loop(0, chunks)
    def _(i):
        add_cross(i)

    cross = acc_x[...]
    cross = jnp.where(core == 0, cross, cross.T).astype(out_x.dtype)
    wide = cross.shape[1] // 2
    out_x[0] = cross[:, :wide].reshape(out_x.shape[1:])
    out_x[1] = cross[:, wide:].reshape(out_x.shape[1:])

    @pl.loop(0, spaces - 1)
    def _(i):
        to = away(i)
        for to_core in range(2):
            send(out_x.at[to_core, to], in_x.at[2 * i + core], 1, to_core, to)

    send(out_x.at[1 - core, space], in_x.at[peers - 2], 1, 1 - core, space)

    landed(in_own, recv_sems.at[0])
    mine = acc[span(space, 16), :]
    diag_ref[core, space] = mine + jnp.sum(in_own[...].astype(jnp.float32), axis=0)

    @pl.loop(0, spaces - 1)
    def _(i):
        send(diag_ref.at[core, space], diag_ref.at[core, space], 2, core, away(i))

    landed(in_x, recv_sems.at[1])
    mine = out_x[core, space].astype(jnp.float32)
    cross_ref[me] = mine + jnp.sum(in_x[...].astype(jnp.float32), axis=0)

    @pl.loop(0, spaces - 1)
    def _(i):
        to = away(i)
        for to_core in range(2):
            send(cross_ref.at[me], cross_ref.at[me], 3, to_core, to)

    send(cross_ref.at[me], cross_ref.at[me], 3, 1 - core, space)

    landed(diag_ref.at[0, pl.ds(0, spaces - 1)], recv_sems.at[2])
    send(diag_ref.at[core], diag_ref.at[core], 4, 1 - core, space)
    landed(cross_ref.at[pl.ds(0, peers - 1)], recv_sems.at[3])
    landed(in_own, send_sems.at[0])
    landed(in_x, send_sems.at[1])
    landed(diag_ref.at[0, pl.ds(0, spaces - 1)], send_sems.at[2])
    landed(cross_ref.at[pl.ds(0, peers - 1)], send_sems.at[3])

    @pl.loop(0, chunks)
    def _(i):
        swap(i).wait_send()

    for sems in (recv_sems, send_sems):
        landed(diag_ref.at[0], sems.at[4])


def subspace_kernel(points, diag_ref, cross_ref, sketch_ref, q_ref, corr_ref, gram):
    k = corr_ref.shape[0]
    cross = cross_ref[...].reshape(k // 16, 2, 16, k // 2)
    corner = jnp.concatenate([cross[:, c].reshape(k, k // 2) for c in range(2)], axis=1)
    gram[:k, :k] = diag_ref[0].reshape(k, k)
    gram[k:, k:] = diag_ref[1].reshape(k, k)
    gram[:k, k:] = corner
    gram[k:, :k] = corner.T
    block = sketch_ref[...].T
    for _ in range(ITERS):
        y = dot(block, gram[...], 1, 0)
        block = dot(inverse_factor(dot(y, y, 1, 1)), y, 1, 0)
    q_b = block.T.astype(jnp.bfloat16)
    q_ref[...] = q_b
    own = pl.multiple_of(lax.rem(lax.axis_index("leaf"), 2) * k, k)
    corr_ref[...] = dot(gram[pl.ds(own, k), :], q_b.astype(jnp.float32), 1, 0) * (1.0 / points)


def fresh_kernel(own_a, own_b, other_a, other_b, q_ref, fresh_ref, held, sem):
    core = lax.rem(lax.axis_index("leaf"), 2)
    half, k = own_a.shape
    own = pl.ds(pl.multiple_of(core * k, k), k)
    rest = pl.ds(pl.multiple_of((1 - core) * k, k), k)
    weights = jnp.concatenate([q_ref[own, :], q_ref[rest, :]], axis=0)
    copies = []
    for part, (mine, other) in enumerate(((own_a, other_b), (own_b, other_a))):
        start = (1 - core if part == 0 else core) * half
        for i in range(half // TILE):
            rows = pl.ds(i * TILE, TILE)
            at = pl.ds(part * half + i * TILE, TILE)
            merged = jnp.concatenate([mine[rows, :], other[rows, :]], axis=1)
            held[at, :] = dot(merged, weights, 1, 0, None).astype(jnp.bfloat16)
            to = fresh_ref.at[0, pl.ds(pl.multiple_of(start + i * TILE, TILE), TILE)]
            copies.append(pltpu.make_async_copy(held.at[at], to, sem.at[len(copies)]))
            copies[-1].start()
    for copy in copies:
        copy.wait()


def from_partner(value, axis, stride):
    return lax.ppermute(value, axis, [(i, i ^ 1 << stride) for i in range(lax.axis_size(axis))])


def on_device(basis, sing_vals, sketch):
    rows, k = basis.shape[1:]
    spaces = lax.axis_size("space")
    points = rows * spaces
    half = rows // 2
    vmem = pl.BlockSpec(memory_space=pltpu.VMEM)
    any_space = pl.BlockSpec(memory_space=pl.ANY)
    f32, wire = jnp.float32, jnp.bfloat16
    chunks = half // CHUNK
    own_a, own_b, other_a, diag, cross = pl.pallas_call(
        exchange_kernel,
        out_shape=(
            pltpu.VMEM((half, k), jnp.bfloat16),
            pltpu.VMEM((half, k), jnp.bfloat16),
            pltpu.VMEM((half, k), jnp.bfloat16),
            pltpu.VMEM((2, spaces, k // spaces, k), f32),
            pltpu.VMEM((2 * spaces, k // spaces, k // 2), f32),
        ),
        in_specs=[pl.BlockSpec(memory_space=pltpu.HBM)] * 2,
        out_specs=(vmem,) * 5,
        scratch_shapes=[
            pltpu.VMEM((1, k), f32),
            pltpu.VMEM((chunks, k, CHUNK), jnp.bfloat16),
            pltpu.VMEM((k, k), f32),
            pltpu.VMEM((k, k), f32),
            pltpu.VMEM((spaces, k // spaces, k), wire),
            pltpu.VMEM((spaces - 1, k // spaces, k), wire),
            pltpu.VMEM((2, spaces, k // spaces, k // 2), wire),
            pltpu.VMEM((2 * spaces - 1, k // spaces, k // 2), wire),
            pltpu.SemaphoreType.REGULAR,
            pltpu.SemaphoreType.REGULAR,
            pltpu.SemaphoreType.DMA,
            pltpu.SemaphoreType.DMA((chunks + half // STRIP,)),
            pltpu.SemaphoreType.DMA((chunks,)),
            pltpu.SemaphoreType.DMA((chunks,)),
            pltpu.SemaphoreType.DMA((5,)),
            pltpu.SemaphoreType.DMA((5,)),
        ],
        compiler_params=pltpu.CompilerParams(
            collective_id=0, has_side_effects=True, vmem_limit_bytes=36 * 2**20
        ),
        name="exchange",
    )(basis, sing_vals)
    other_b = from_partner(own_b, "leaf", 0)
    block_b, correlation = pl.pallas_call(
        functools.partial(subspace_kernel, points),
        out_shape=(
            jax.ShapeDtypeStruct(sketch.shape, jnp.bfloat16),
            jax.ShapeDtypeStruct((k, k), f32),
        ),
        in_specs=[vmem, vmem, vmem],
        out_specs=(vmem, vmem),
        scratch_shapes=[pltpu.VMEM((2 * k, 2 * k), f32)],
        compiler_params=pltpu.CompilerParams(vmem_limit_bytes=16 * 2**20),
        cost_estimate=pl.CostEstimate(flops=2**31, bytes_accessed=80 * 2**20, transcendentals=0),
        name="subspace",
    )(diag, cross, sketch)
    fresh = pl.pallas_call(
        fresh_kernel,
        out_shape=jax.ShapeDtypeStruct((1, rows, k), jnp.bfloat16),
        in_specs=[vmem] * 5,
        out_specs=any_space,
        scratch_shapes=[
            pltpu.VMEM((rows, k), jnp.bfloat16),
            pltpu.SemaphoreType.DMA((rows // TILE,)),
        ],
        compiler_params=pltpu.CompilerParams(vmem_limit_bytes=32 * 2**20),
        name="fresh",
    )(own_a, own_b, other_a, other_b, block_b)
    return (fresh, correlation[None])


def solution(mesh):
    in_specs = (P("leaf", "space", None), P("leaf", None), P())
    out_specs = (P("leaf", "space", None), P("leaf", None, None))
    return jax.shard_map(
        on_device, mesh=mesh, in_specs=in_specs, out_specs=out_specs, check_vma=False
    )
```

time: 58.4 us -> 51.4 us (0.88)
  Pallas kernels: 56.3 us -> 49.2 us
    pallas_call x1, Pallas kernels: 29.2 us -> 25.5 us  [on_device(): pl.pallas_call(exchange_kernel, out_shape=(pltpu.VMEM((half, k), jnp.bflo...]
    pallas_call x1, Pallas kernels: 20.8 us -> 17.3 us  [on_device(): pl.pallas_call(functools.partial(subspace_kernel, points), out_shape=(jax...]
  transfers between devices with their start and end apart: 1 -> 1, of which waited for: 0 -> 0; matrix products, arithmetic and copies ran while one was open for 0% -> 0% of each run, Pallas kernels for 36% -> 34%
where the time goes in v4:
time: 51.4 us; the launch traced here: 51.3 us
  Pallas kernels  49.2 us (96%)
  between operations  0.81 us (2%)
  local copies, waits for them, and re-layouts  0.68 us (1%)
  starting transfers between devices  0.6 us (1%)
    pallas_call x1, Pallas kernels, on_device(): pl.pallas_call(exchange_kernel, out_shape=(pltpu.VMEM((half, k), jnp.bflo...  25.5 us
    pallas_call x1, Pallas kernels, on_device(): pl.pallas_call(functools.partial(subspace_kernel, points), out_shape=(jax...  17.3 us
    pallas_call x1, Pallas kernels, on_device(): pl.pallas_call(fresh_kernel, out_shape=jax.ShapeDtypeStruct((1, rows, k),...  6.47 us
  transfers between devices with their start and end apart: 1, of which 0 were waited for; matrix products, arithmetic and copies ran while one was open for 0% of the time, Pallas kernels for 34%

profile of v4, /device:TPU:1, one launch (start us, length us, event | category | flops | bytes accessed | tf_op | source)
XLA Modules:
  0.0 51.3 jit_solution(17480514314460050425)
XLA Ops:
  0.6 0.0 copy-start
  0.6 0.7 %copy-done = f32[1,256]{1,0:T(1,128)S(1)} copy-done((f32[1,256]{1,0:T(1,128)S(1)}, f32[1,256]{1,0:T(1,128)}, u32[]{:S(2)}) %copy-start) | copy-done | bytes 1048
  1.3 0.0 copy-start.1
  1.3 25.5 %exchange.1 = (bf16[8192,256]{1,0:T(8,128)(2,1)S(1)}, bf16[8192,256]{1,0:T(8,128)(2,1)S(1)}, bf16[8192,256]{1,0:T(8,128)(2,1)S(1)}, f32[2,16,16,256]{3,2,1,0:T(8,128)S(1)}, f32[32,16,128]{2,1,0:T(8,128)S(1)}) custom-call(bf16[1,16384,256]{2,1,0:T(8,128)(2,1)} %basis_ref.1, f32[1,256]{1,0:T(1,128)S(1)} %copy-done), custom_call_target="tpu_custom_call" | custom-call | tf_op jit(solution)/shard_map/exchange/pallas_call | solution.py:339
  26.8 0.6 %collective-permute-start = (bf16[8192,256]{1,0:T(8,128)(2,1)S(1)}, bf16[8192,256]{1,0:T(8,128)(2,1)S(1)}, u32[]{:S(2)}, u32[]{:S(2)}) collective-permute-start(bf16[8192,256]{1,0:T(8,128)(2,1)S(1)} %get-tuple-element.10.own_b), channel_id=1, source_target_pairs={{0,16},{16,0},{32,48},{48,32},{64,80},{80,64},{96,112},{112,96},{1... | collective-permute-start | bytes 12582920 | tf_op jit(solution)/shard_map/ppermute | solution.py:327
  27.4 0.0 copy-done.1
  27.4 17.3 %subspace.1 = (bf16[512,256]{1,0:T(8,128)(2,1)S(1)}, f32[256,256]{1,0:T(8,128)}) custom-call(f32[2,16,16,256]{3,2,1,0:T(8,128)S(1)} %get-tuple-element.12.diag_ref, f32[32,16,128]{2,1,0:T(8,128)S(1)} %get-tuple-element.13.cross_ref, f32[512,256]{1,0:T(8,128)S(1)} %copy-done.1), custom_call_target="tpu_custom_call" | custom-call | flops 2147483648 | bytes 83886080 | tf_op jit(solution)/shard_map/subspace/pallas_call | solution.py:374
  44.7 0.0 collective-permute-done.other_b
  44.7 6.5 %fresh.1 = bf16[1,16384,256]{2,1,0:T(8,128)(2,1)} custom-call(bf16[8192,256]{1,0:T(8,128)(2,1)S(1)} %get-tuple-element.9.own_a, bf16[8192,256]{1,0:T(8,128)(2,1)S(1)} %get-tuple-element.10.own_b, bf16[8192,256]{1,0:T(8,128)(2,1)S(1)} %get-tuple-element.11.other_a, bf16[8192,256]{1,0:T(8,128)(2,1)S(1)} %collective-permute-done.other_b, ...), custom_call_target="tpu_custom_call" | custom-call | tf_op jit(solution)/shard_map/fresh/pallas_call | solution.py:387
Async XLA Ops:
  0.6 0.7 %copy-start = (f32[1,256]{1,0:T(1,128)S(1)}, f32[1,256]{1,0:T(1,128)}, u32[]{:S(2)}) copy-start(f32[1,256]{1,0:T(1,128)} %sing_ref.1) | copy-start | bytes 3076
  1.3 26.1 %copy-start.1 = (f32[512,256]{1,0:T(8,128)S(1)}, f32[512,256]{1,0:T(8,128)}, u32[]{:S(2)}) copy-start(f32[512,256]{1,0:T(8,128)} %sketch_ref.1) | copy-start | bytes 1572868
  26.8 17.9 %collective-permute-start = (bf16[8192,256]{1,0:T(8,128)(2,1)S(1)}, bf16[8192,256]{1,0:T(8,128)(2,1)S(1)}, u32[]{:S(2)}, u32[]{:S(2)}) collective-permute-start(bf16[8192,256]{1,0:T(8,128)(2,1)S(1)} %get-tuple-element.10.own_b), channel_id=1, source_target_pairs={{0,16},{16,0},{32,48},{48,32},{64,80},{80,64},{96,112},{112,96},{1... | collective-permute-start | bytes 12582920 | tf_op jit(solution)/shard_map/ppermute | solution.py:327

commit v5 on v4

--- a/solution.py
+++ b/solution.py
@@ -11,7 +11,7 @@
 SUB = 16
 CHUNK = 1024
 STRIP = 2048
-TILE = 2048
+TILE = 512
 MESH = pl.DeviceIdType.MESH
 EXACT = lax.Precision.HIGH
 
@@ -93,10 +93,11 @@
         done.append(jnp.where(lane_wide < after, block, 0.0))
         blank = (lane_wide >= first) & (lane_wide < after)
         left, right = stack(block)
-        near = dot(left[:, after : after + PANEL], right, 0, 0, None)
+        turned = [left[:, 128 * h : 128 * h + 128].T for h in range(wide)]
+        near = dot(turned[after // 128][after % 128 : after % 128 + PANEL], right, 1, 0, None)
         panels[p + 1] = jnp.where(blank, 0.0, panels[p + 1]) - near
         if after + PANEL < n:
-            far = dot(left[:, after + PANEL :], right, 0, 0, None)
+            far = dot(jnp.concatenate(turned, axis=0)[after + PANEL :], right, 1, 0, None)
             for m in range(p + 2, count):
                 at = (m - p - 2) * PANEL
                 panels[m] = jnp.where(blank, 0.0, panels[m]) - far[at : at + PANEL]
@@ -104,9 +105,9 @@
 
 
 def exchange_kernel(
-    basis_ref, sing_ref, own_a, own_b, other_a, diag_ref, cross_ref,
-    sing, turned, acc, acc_x, out_own, in_own, out_x, in_x,
-    answer, entered, sing_sem, load_sem, swap_send, swap_recv, send_sems, recv_sems,
+    basis_ref, sing_ref, own_a, own_b, other_a, other_b, diag_ref, cross_ref,
+    turned, acc, acc_x, out_own, in_own, out_x, in_x,
+    answer, entered, load_sem, swap_send, swap_recv, rest_sems, send_sems, recv_sems,
 ):
     leaf, space = lax.axis_index("leaf"), lax.axis_index("space")
     spaces = lax.axis_size("space")
@@ -135,7 +136,7 @@
 
     def scale(part, i, size):
         rows = span(i, size)
-        part[rows, :] = (part[rows, :].astype(jnp.float32) * sing[...]).astype(jnp.bfloat16)
+        part[rows, :] = (part[rows, :].astype(jnp.float32) * sing_ref[...]).astype(jnp.bfloat16)
 
     def swap(i):
         return pltpu.make_async_remote_copy(
@@ -144,6 +145,11 @@
             device_id=partner, device_id_type=MESH,
         )
 
+    swap_rest = pltpu.make_async_remote_copy(
+        src_ref=own_b, dst_ref=other_b, send_sem=rest_sems.at[0], recv_sem=rest_sems.at[1],
+        device_id=partner, device_id_type=MESH,
+    )
+
     def send(src, dst, which, to_core, to_space):
         pltpu.make_async_remote_copy(
             src_ref=src, dst_ref=dst, send_sem=send_sems.at[which], recv_sem=recv_sems.at[which],
@@ -153,8 +159,6 @@
     def landed(ref, sem):
         pltpu.make_async_copy(ref, ref, sem).wait()
 
-    sing_copy = pltpu.make_async_copy(sing_ref, sing, sing_sem)
-    sing_copy.start()
     first, second = (1 - core) * half, core * half
     for i in range(chunks):
         load(own_a, first, i, CHUNK, load_sem.at[i]).start()
@@ -184,7 +188,6 @@
 
     acc[...] = jnp.zeros_like(acc)
     acc_x[...] = jnp.zeros_like(acc_x)
-    sing_copy.wait()
     load(own_a, first, 0, CHUNK, load_sem.at[0]).wait()
     scale(own_a, 0, CHUNK)
     swap(0).start()
@@ -234,8 +237,8 @@
     def _(i):
         add_cross(i)
 
-    cross = acc_x[...]
-    cross = jnp.where(core == 0, cross, cross.T).astype(out_x.dtype)
+    cross = acc_x[...].astype(out_x.dtype)
+    cross = jnp.where(core == 0, cross, cross.T)
     wide = cross.shape[1] // 2
     out_x[0] = cross[:, :wide].reshape(out_x.shape[1:])
     out_x[1] = cross[:, wide:].reshape(out_x.shape[1:])
@@ -248,6 +251,8 @@
 
     send(out_x.at[1 - core, space], in_x.at[peers - 2], 1, 1 - core, space)
 
+    swap_rest.start()
+
     landed(in_own, recv_sems.at[0])
     mine = acc[span(space, 16), :]
     diag_ref[core, space] = mine + jnp.sum(in_own[...].astype(jnp.float32), axis=0)
@@ -258,7 +263,8 @@
 
     landed(in_x, recv_sems.at[1])
     mine = out_x[core, space].astype(jnp.float32)
-    cross_ref[me] = mine + jnp.sum(in_x[...].astype(jnp.float32), axis=0)
+    total = mine + jnp.sum(in_x[...].astype(jnp.float32), axis=0)
+    cross_ref[me] = total.astype(cross_ref.dtype)
 
     @pl.loop(0, spaces - 1)
     def _(i):
@@ -280,13 +286,14 @@
     def _(i):
         swap(i).wait_send()
 
+    swap_rest.wait()
     for sems in (recv_sems, send_sems):
         landed(diag_ref.at[0], sems.at[4])
 
 
 def subspace_kernel(points, diag_ref, cross_ref, sketch_ref, q_ref, corr_ref, gram):
     k = corr_ref.shape[0]
-    cross = cross_ref[...].reshape(k // 16, 2, 16, k // 2)
+    cross = cross_ref[...].astype(jnp.float32).reshape(k // 16, 2, 16, k // 2)
     corner = jnp.concatenate([cross[:, c].reshape(k, k // 2) for c in range(2)], axis=1)
     gram[:k, :k] = diag_ref[0].reshape(k, k)
     gram[k:, k:] = diag_ref[1].reshape(k, k)
@@ -323,10 +330,6 @@
         copy.wait()
 
 
-def from_partner(value, axis, stride):
-    return lax.ppermute(value, axis, [(i, i ^ 1 << stride) for i in range(lax.axis_size(axis))])
-
-
 def on_device(basis, sing_vals, sketch):
     rows, k = basis.shape[1:]
     spaces = lax.axis_size("space")
@@ -336,19 +339,19 @@
     any_space = pl.BlockSpec(memory_space=pl.ANY)
     f32, wire = jnp.float32, jnp.bfloat16
     chunks = half // CHUNK
-    own_a, own_b, other_a, diag, cross = pl.pallas_call(
+    own_a, own_b, other_a, other_b, diag, cross = pl.pallas_call(
         exchange_kernel,
         out_shape=(
             pltpu.VMEM((half, k), jnp.bfloat16),
             pltpu.VMEM((half, k), jnp.bfloat16),
             pltpu.VMEM((half, k), jnp.bfloat16),
+            pltpu.VMEM((half, k), jnp.bfloat16),
             pltpu.VMEM((2, spaces, k // spaces, k), f32),
-            pltpu.VMEM((2 * spaces, k // spaces, k // 2), f32),
+            pltpu.VMEM((2 * spaces, k // spaces, k // 2), wire),
         ),
-        in_specs=[pl.BlockSpec(memory_space=pltpu.HBM)] * 2,
-        out_specs=(vmem,) * 5,
+        in_specs=[pl.BlockSpec(memory_space=pltpu.HBM), vmem],
+        out_specs=(vmem,) * 6,
         scratch_shapes=[
-            pltpu.VMEM((1, k), f32),
             pltpu.VMEM((chunks, k, CHUNK), jnp.bfloat16),
             pltpu.VMEM((k, k), f32),
             pltpu.VMEM((k, k), f32),
@@ -358,10 +361,10 @@
             pltpu.VMEM((2 * spaces - 1, k // spaces, k // 2), wire),
             pltpu.SemaphoreType.REGULAR,
             pltpu.SemaphoreType.REGULAR,
-            pltpu.SemaphoreType.DMA,
             pltpu.SemaphoreType.DMA((chunks + half // STRIP,)),
             pltpu.SemaphoreType.DMA((chunks,)),
             pltpu.SemaphoreType.DMA((chunks,)),
+            pltpu.SemaphoreType.DMA((2,)),
             pltpu.SemaphoreType.DMA((5,)),
             pltpu.SemaphoreType.DMA((5,)),
         ],
@@ -370,7 +373,6 @@
         ),
         name="exchange",
     )(basis, sing_vals)
-    other_b = from_partner(own_b, "leaf", 0)
     block_b, correlation = pl.pallas_call(
         functools.partial(subspace_kernel, points),
         out_shape=(

time: 51.4 us -> 48.6 us (0.946)
  Pallas kernels: 49.2 us -> 47 us
  starting transfers between devices: 0.6 us -> 0 us
    pallas_call x1, Pallas kernels: 25.5 us -> 24.3 us  [on_device(): pl.pallas_call(exchange_kernel, out_shape=(pltpu.VMEM((half, k), jnp.bflo...]
    pallas_call x1, Pallas kernels: 17.3 us -> 16.5 us  [on_device(): pl.pallas_call(functools.partial(subspace_kernel, points), out_shape=(jax...]
    ppermute x1 -> x0, starting transfers between devices: 0.6 us -> none  [from_partner(): lax.ppermute(value, axis, [(i, i ^ 1 << stride) for i in range(lax.axis_s...]
  transfers between devices with their start and end apart: 1 -> 0, of which waited for: 0 -> 0; matrix products, arithmetic and copies ran while one was open for 0% -> 0% of each run, Pallas kernels for 34% -> 0%
where the time goes in v5:
time: 48.6 us; the launch traced here: 48.5 us
  Pallas kernels  47 us (97%)
  between operations  0.82 us (2%)
  local copies, waits for them, and re-layouts  0.68 us (1%)
    pallas_call x1, Pallas kernels, on_device(): pl.pallas_call(exchange_kernel, out_shape=(pltpu.VMEM((half, k), jnp.bflo...  24.3 us
    pallas_call x1, Pallas kernels, on_device(): pl.pallas_call(functools.partial(subspace_kernel, points), out_shape=(jax...  16.5 us
    pallas_call x1, Pallas kernels, on_device(): pl.pallas_call(fresh_kernel, out_shape=jax.ShapeDtypeStruct((1, rows, k),...  6.2 us

profile of v5, /device:TPU:1, one launch (start us, length us, event | category | flops | bytes accessed | tf_op | source)
XLA Modules:
  0.0 48.5 jit_solution(5631680439559150641)
XLA Ops:
  0.6 0.0 copy-start
  0.6 0.7 %copy-done = f32[1,256]{1,0:T(1,128)S(1)} copy-done((f32[1,256]{1,0:T(1,128)S(1)}, f32[1,256]{1,0:T(1,128)}, u32[]{:S(2)}) %copy-start) | copy-done | bytes 1048
  1.3 0.0 copy-start.1
  1.3 24.3 %exchange.1 = (bf16[8192,256]{1,0:T(8,128)(2,1)S(1)}, bf16[8192,256]{1,0:T(8,128)(2,1)S(1)}, bf16[8192,256]{1,0:T(8,128)(2,1)S(1)}, bf16[8192,256]{1,0:T(8,128)(...) custom-call(bf16[1,16384,256]{2,1,0:T(8,128)(2,1)} %basis_ref.1, f32[1,256]{1,0:T(1,128)S(1)} %copy-done), custom_call_target="tpu_custom_call" | custom-call | tf_op jit(solution)/shard_map/exchange/pallas_call | solution.py:342
  25.6 0.0 copy-done.1
  25.6 16.5 %subspace.1 = (bf16[512,256]{1,0:T(8,128)(2,1)S(1)}, f32[256,256]{1,0:T(8,128)}) custom-call(f32[2,16,16,256]{3,2,1,0:T(8,128)S(1)} %get-tuple-element.14.diag_ref, bf16[32,16,128]{2,1,0:T(8,128)(2,1)S(1)} %get-tuple-element.15.cross_ref, f32[512,256]{1,0:T(8,128)S(1)} %copy-done.1), custom_call_target="tpu_custom_call" | custom-call | flops 2147483648 | bytes 83886080 | tf_op jit(solution)/shard_map/subspace/pallas_call | solution.py:376
  42.1 6.2 %fresh.1 = bf16[1,16384,256]{2,1,0:T(8,128)(2,1)} custom-call(bf16[8192,256]{1,0:T(8,128)(2,1)S(1)} %get-tuple-element.10.own_a, bf16[8192,256]{1,0:T(8,128)(2,1)S(1)} %get-tuple-element.11.own_b, bf16[8192,256]{1,0:T(8,128)(2,1)S(1)} %get-tuple-element.12.other_a, bf16[8192,256]{1,0:T(8,128)(2,1)S(1)} %get-tuple-element.13.other_b, ...), custom_call_target="tpu_custom_call" | custom-call | tf_op jit(solution)/shard_map/fresh/pallas_call | solution.py:389
Async XLA Ops:
  0.6 0.7 %copy-start = (f32[1,256]{1,0:T(1,128)S(1)}, f32[1,256]{1,0:T(1,128)}, u32[]{:S(2)}) copy-start(f32[1,256]{1,0:T(1,128)} %sing_ref.1) | copy-start | bytes 3076
  1.3 24.3 %copy-start.1 = (f32[512,256]{1,0:T(8,128)S(1)}, f32[512,256]{1,0:T(8,128)}, u32[]{:S(2)}) copy-start(f32[512,256]{1,0:T(8,128)} %sketch_ref.1) | copy-start | bytes 1572868

commit v6 on v5

--- a/solution.py
+++ b/solution.py
@@ -9,8 +9,8 @@
 ITERS = 2
 PANEL = 32
 SUB = 16
-CHUNK = 1024
-STRIP = 2048
+CHUNK = 2048
+STRIP = 4096
 TILE = 512
 MESH = pl.DeviceIdType.MESH
 EXACT = lax.Precision.HIGH
@@ -40,6 +40,14 @@
     row = lax.broadcasted_iota(jnp.int32, tile, 0)
     lane_wide = lax.broadcasted_iota(jnp.int32, (PANEL, n), 1)
     unit = [jnp.where(row == s, 1.0, 0.0) for s in range(8)]
+    shrink, grow = [], []
+    for h in range(wide):
+        corner = inner[128 * h : 128 * h + 128, 128 * h : 128 * h + 128]
+        square = [lax.broadcasted_iota(jnp.int32, (128, 128), axis) for axis in range(2)]
+        spots = jnp.sum(jnp.where(square[0] == square[1], corner, 0.0), axis=0, keepdims=True)
+        spots = jnp.broadcast_to(spots, tile)
+        shrink.append(lax.rsqrt(spots))
+        grow.append(spots * shrink[h])
     panels = [inner[i * PANEL : (i + 1) * PANEL] for i in range(count)]
     done = []
     for p in range(count):
@@ -51,34 +59,44 @@
         ]
         diag = [jnp.zeros(tile, jnp.float32)] * tall
         for sub in range(0, PANEL, SUB):
+            near_cols = {r: w[r][here] * shrink[here] for r in range(sub // 8, tall)}
+            spots = [base + sub + j for j in range(SUB)]
             cols = [
-                {
-                    r: jnp.broadcast_to(w[r][here][:, base + sub + j : base + sub + j + 1], tile)
-                    for r in range(sub // 8, tall)
-                }
-                for j in range(SUB)
+                {r: jnp.broadcast_to(value[:, at : at + 1], tile) for r, value in near_cols.items()}
+                for at in spots
             ]
-            for j in range(SUB):
+            back = [jnp.broadcast_to(grow[here][:, at : at + 1], tile) for at in spots]
+            for j in range(0, SUB, 2):
                 at = sub + j
                 top, s = at // 8, at % 8
-                inv = 1.0 / jnp.broadcast_to(cols[j][top][s : s + 1], tile)
-                mult = {r: cols[j][r] * inv for r in range(top, tall)}
-                mult[top] = jnp.where(row > s, mult[top], 0.0)
-                if s == 7:
-                    del mult[top]
-                for k in range(j + 1, SUB):
-                    pivot = cols[k][top][s : s + 1]
-                    for r in mult:
-                        cols[k][r] = cols[k][r] - mult[r] * pivot
-                diag[top] = jnp.where(row == s, cols[j][top], diag[top])
-                at_lane = lane == base + at
-                w[top][here] = jnp.where(at_lane, unit[s], w[top][here])
-                for r in range(top + 1, tall):
-                    w[r][here] = jnp.where(at_lane, 0.0, w[r][here])
+                one, two = cols[j], cols[j + 1]
+                a, b = (jnp.broadcast_to(one[top][s + t : s + t + 1], tile) for t in range(2))
+                c, d = (jnp.broadcast_to(two[top][s + t : s + t + 1], tile) for t in range(2))
+                det = a * d - b * c
+                inv_det, inv_a = 1.0 / det, 1.0 / a
+                left = {r: (d * one[r] - b * two[r]) * inv_det for r in range(top, tall)}
+                right = {r: (a * two[r] - c * one[r]) * inv_det for r in range(top, tall)}
+                left[top] = jnp.where(row > s + 1, left[top], 0.0)
+                right[top] = jnp.where(row > s + 1, right[top], 0.0)
+                if s == 6:
+                    del left[top], right[top]
+                for k in range(j + 2, SUB):
+                    e, f = cols[k][top][s : s + 1], cols[k][top][s + 1 : s + 2]
+                    for r in left:
+                        cols[k][r] = (cols[k][r] - left[r] * e) - right[r] * f
+                diag[top] = jnp.where(row == s, a * back[j], diag[top])
+                diag[top] = jnp.where(row == s + 1, det * inv_a * back[j + 1], diag[top])
+                for t in range(2):
+                    at_lane = lane == base + at + t
+                    w[top][here] = jnp.where(at_lane, unit[s + t], w[top][here])
+                    for r in range(top + 1, tall):
+                        w[r][here] = jnp.where(at_lane, 0.0, w[r][here])
+                low = jnp.where(row == s + 1, b * inv_a, 0.0)
                 for h in range(wide):
-                    pivot = w[top][h][s : s + 1]
-                    for r in mult:
-                        w[r][h] = w[r][h] - mult[r] * pivot
+                    e, f = w[top][h][s : s + 1], w[top][h][s + 1 : s + 2]
+                    for r in left:
+                        w[r][h] = (w[r][h] - left[r] * e) - right[r] * f
+                    w[top][h] = w[top][h] - low * e
         for r in range(tall):
             scale = lax.rsqrt(diag[r])
             w[r] = [value * scale for value in w[r]]
@@ -92,12 +110,12 @@
             break
         done.append(jnp.where(lane_wide < after, block, 0.0))
         blank = (lane_wide >= first) & (lane_wide < after)
-        left, right = stack(block)
-        turned = [left[:, 128 * h : 128 * h + 128].T for h in range(wide)]
-        near = dot(turned[after // 128][after % 128 : after % 128 + PANEL], right, 1, 0, None)
+        stacked, terms = stack(block)
+        turned = [stacked[:, 128 * h : 128 * h + 128].T for h in range(wide)]
+        near = dot(turned[after // 128][after % 128 : after % 128 + PANEL], terms, 1, 0, None)
         panels[p + 1] = jnp.where(blank, 0.0, panels[p + 1]) - near
         if after + PANEL < n:
-            far = dot(jnp.concatenate(turned, axis=0)[after + PANEL :], right, 1, 0, None)
+            far = dot(jnp.concatenate(turned, axis=0)[after + PANEL :], terms, 1, 0, None)
             for m in range(p + 2, count):
                 at = (m - p - 2) * PANEL
                 panels[m] = jnp.where(blank, 0.0, panels[m]) - far[at : at + PANEL]

time: 48.6 us -> 47.5 us (0.977)
  Pallas kernels: 47 us -> 45.9 us
    pallas_call x1, Pallas kernels: 24.3 us -> 23.4 us  [on_device(): pl.pallas_call(exchange_kernel, out_shape=(pltpu.VMEM((half, k), jnp.bflo...]
where the time goes in v6:
time: 47.5 us; the launch traced here: 47.4 us
  Pallas kernels  45.9 us (97%)
  between operations  0.84 us (2%)
  local copies, waits for them, and re-layouts  0.68 us (1%)
    pallas_call x1, Pallas kernels, on_device(): pl.pallas_call(exchange_kernel, out_shape=(pltpu.VMEM((half, k), jnp.bflo...  23.4 us
    pallas_call x1, Pallas kernels, on_device(): pl.pallas_call(functools.partial(subspace_kernel, points), out_shape=(jax...  16.2 us
    pallas_call x1, Pallas kernels, on_device(): pl.pallas_call(fresh_kernel, out_shape=jax.ShapeDtypeStruct((1, rows, k),...  6.25 us

profile of v6, /device:TPU:1, one launch (start us, length us, event | category | flops | bytes accessed | tf_op | source)
XLA Modules:
  0.0 47.4 jit_solution(1171223584912493178)
XLA Ops:
  0.6 0.0 copy-start
  0.6 0.7 %copy-done = f32[1,256]{1,0:T(1,128)S(1)} copy-done((f32[1,256]{1,0:T(1,128)S(1)}, f32[1,256]{1,0:T(1,128)}, u32[]{:S(2)}) %copy-start) | copy-done | bytes 1048
  1.3 0.0 copy-start.1
  1.3 23.4 %exchange.1 = (bf16[8192,256]{1,0:T(8,128)(2,1)S(1)}, bf16[8192,256]{1,0:T(8,128)(2,1)S(1)}, bf16[8192,256]{1,0:T(8,128)(2,1)S(1)}, bf16[8192,256]{1,0:T(8,128)(...) custom-call(bf16[1,16384,256]{2,1,0:T(8,128)(2,1)} %basis_ref.1, f32[1,256]{1,0:T(1,128)S(1)} %copy-done), custom_call_target="tpu_custom_call" | custom-call | tf_op jit(solution)/shard_map/exchange/pallas_call | solution.py:360
  24.7 0.0 copy-done.1
  24.7 16.2 %subspace.1 = (bf16[512,256]{1,0:T(8,128)(2,1)S(1)}, f32[256,256]{1,0:T(8,128)}) custom-call(f32[2,16,16,256]{3,2,1,0:T(8,128)S(1)} %get-tuple-element.14.diag_ref, bf16[32,16,128]{2,1,0:T(8,128)(2,1)S(1)} %get-tuple-element.15.cross_ref, f32[512,256]{1,0:T(8,128)S(1)} %copy-done.1), custom_call_target="tpu_custom_call" | custom-call | flops 2147483648 | bytes 83886080 | tf_op jit(solution)/shard_map/subspace/pallas_call | solution.py:394
  41.0 6.3 %fresh.1 = bf16[1,16384,256]{2,1,0:T(8,128)(2,1)} custom-call(bf16[8192,256]{1,0:T(8,128)(2,1)S(1)} %get-tuple-element.10.own_a, bf16[8192,256]{1,0:T(8,128)(2,1)S(1)} %get-tuple-element.11.own_b, bf16[8192,256]{1,0:T(8,128)(2,1)S(1)} %get-tuple-element.12.other_a, bf16[8192,256]{1,0:T(8,128)(2,1)S(1)} %get-tuple-element.13.other_b, ...), custom_call_target="tpu_custom_call" | custom-call | tf_op jit(solution)/shard_map/fresh/pallas_call | solution.py:407
Async XLA Ops:
  0.6 0.7 %copy-start = (f32[1,256]{1,0:T(1,128)S(1)}, f32[1,256]{1,0:T(1,128)}, u32[]{:S(2)}) copy-start(f32[1,256]{1,0:T(1,128)} %sing_ref.1) | copy-start | bytes 3076
  1.3 23.4 %copy-start.1 = (f32[512,256]{1,0:T(8,128)S(1)}, f32[512,256]{1,0:T(8,128)}, u32[]{:S(2)}) copy-start(f32[512,256]{1,0:T(8,128)} %sketch_ref.1) | copy-start | bytes 1572868

commit v7 on v6

--- a/solution.py
+++ b/solution.py
@@ -309,25 +309,44 @@
         landed(diag_ref.at[0], sems.at[4])
 
 
-def subspace_kernel(points, diag_ref, cross_ref, sketch_ref, q_ref, corr_ref, gram):
+def subspace_kernel(points, diag_ref, cross_ref, sketch_ref, q_ref, corr_ref, high, low):
     k = corr_ref.shape[0]
     cross = cross_ref[...].astype(jnp.float32).reshape(k // 16, 2, 16, k // 2)
     corner = jnp.concatenate([cross[:, c].reshape(k, k // 2) for c in range(2)], axis=1)
-    gram[:k, :k] = diag_ref[0].reshape(k, k)
-    gram[k:, k:] = diag_ref[1].reshape(k, k)
-    gram[:k, k:] = corner
-    gram[k:, :k] = corner.T
+    corner = corner.astype(jnp.bfloat16)
+    high[:k, k:] = corner
+    high[k:, :k] = corner.T
+    for at in range(2):
+        own = slice(at * k, at * k + k)
+        whole = diag_ref[at].reshape(k, k)
+        upper = whole.astype(jnp.bfloat16)
+        high[own, own] = upper
+        low[at] = (whole - upper.astype(jnp.float32)).astype(jnp.bfloat16)
+
+    def times_gram(block):
+        upper = block.astype(jnp.bfloat16)
+        lower = (block - upper.astype(jnp.float32)).astype(jnp.bfloat16)
+        small = [dot(upper[:, at * k : at * k + k], low[at], 1, 0, None) for at in range(2)]
+        rest = dot(lower, high[...], 1, 0, None) + jnp.concatenate(small, axis=1)
+        return dot(upper, high[...], 1, 0, None) + rest
+
     block = sketch_ref[...].T
     for _ in range(ITERS):
-        y = dot(block, gram[...], 1, 0)
+        y = times_gram(block)
         block = dot(inverse_factor(dot(y, y, 1, 1)), y, 1, 0)
     q_b = block.T.astype(jnp.bfloat16)
     q_ref[...] = q_b
-    own = pl.multiple_of(lax.rem(lax.axis_index("leaf"), 2) * k, k)
-    corr_ref[...] = dot(gram[pl.ds(own, k), :], q_b.astype(jnp.float32), 1, 0) * (1.0 / points)
-
-
-def fresh_kernel(own_a, own_b, other_a, other_b, q_ref, fresh_ref, held, sem):
+    at = lax.rem(lax.axis_index("leaf"), 2)
+    own = pl.ds(pl.multiple_of(at * k, k), k)
+    term = dot(high[own, :], q_b, 1, 0, None) + dot(low[at], q_ref[own, :], 1, 0, None)
+    corr_ref[...] = term * (1.0 / points)
+
+
+def fresh_kernel(
+    own_a, own_b, other_a, other_b, q_ref, corr_in, fresh_ref, corr_ref, held, sem, corr_sem
+):
+    corr_copy = pltpu.make_async_copy(corr_in, corr_ref.at[0], corr_sem)
+    corr_copy.start()
     core = lax.rem(lax.axis_index("leaf"), 2)
     half, k = own_a.shape
     own = pl.ds(pl.multiple_of(core * k, k), k)
@@ -346,6 +365,7 @@
             copies[-1].start()
     for copy in copies:
         copy.wait()
+    corr_copy.wait()
 
 
 def on_device(basis, sing_vals, sketch):
@@ -395,28 +415,34 @@
         functools.partial(subspace_kernel, points),
         out_shape=(
             jax.ShapeDtypeStruct(sketch.shape, jnp.bfloat16),
-            jax.ShapeDtypeStruct((k, k), f32),
+            pltpu.VMEM((k, k), f32),
         ),
         in_specs=[vmem, vmem, vmem],
         out_specs=(vmem, vmem),
-        scratch_shapes=[pltpu.VMEM((2 * k, 2 * k), f32)],
+        scratch_shapes=[
+            pltpu.VMEM((2 * k, 2 * k), jnp.bfloat16),
+            pltpu.VMEM((2, k, k), jnp.bfloat16),
+        ],
         compiler_params=pltpu.CompilerParams(vmem_limit_bytes=16 * 2**20),
         cost_estimate=pl.CostEstimate(flops=2**31, bytes_accessed=80 * 2**20, transcendentals=0),
         name="subspace",
     )(diag, cross, sketch)
-    fresh = pl.pallas_call(
+    return pl.pallas_call(
         fresh_kernel,
-        out_shape=jax.ShapeDtypeStruct((1, rows, k), jnp.bfloat16),
-        in_specs=[vmem] * 5,
-        out_specs=any_space,
+        out_shape=(
+            jax.ShapeDtypeStruct((1, rows, k), jnp.bfloat16),
+            jax.ShapeDtypeStruct((1, k, k), f32),
+        ),
+        in_specs=[vmem] * 6,
+        out_specs=(any_space, any_space),
         scratch_shapes=[
             pltpu.VMEM((rows, k), jnp.bfloat16),
             pltpu.SemaphoreType.DMA((rows // TILE,)),
+            pltpu.SemaphoreType.DMA,
         ],
         compiler_params=pltpu.CompilerParams(vmem_limit_bytes=32 * 2**20),
         name="fresh",
-    )(own_a, own_b, other_a, other_b, block_b)
-    return (fresh, correlation[None])
+    )(own_a, own_b, other_a, other_b, block_b, correlation)
 
 
 def solution(mesh):

time: 47.5 us -> 46.6 us (0.981)
  Pallas kernels: 45.9 us -> 44.9 us
    pallas_call x1, Pallas kernels: 16.2 us -> 15.2 us  [on_device(): pl.pallas_call(functools.partial(subspace_kernel, points), out_shape=(jax...]
where the time goes in v7:
time: 46.6 us; the launch traced here: 46.4 us
  Pallas kernels  44.9 us (96%)
  between operations  0.84 us (2%)
  local copies, waits for them, and re-layouts  0.68 us (1%)
    pallas_call x1, Pallas kernels, on_device(): pl.pallas_call(exchange_kernel, out_shape=(pltpu.VMEM((half, k), jnp.bflo...  23.4 us
    pallas_call x1, Pallas kernels, on_device(): pl.pallas_call(functools.partial(subspace_kernel, points), out_shape=(jax...  15.2 us
    pallas_call x1, Pallas kernels, on_device(): pl.pallas_call(fresh_kernel, out_shape=(jax.ShapeDtypeStruct((1, rows, k)...  6.28 us

profile of v7, /device:TPU:1, one launch (start us, length us, event | category | flops | bytes accessed | tf_op | source)
XLA Modules:
  0.0 46.4 jit_solution(18299494094846757685)
XLA Ops:
  0.6 0.0 copy-start
  0.6 0.7 %copy-done = f32[1,256]{1,0:T(1,128)S(1)} copy-done((f32[1,256]{1,0:T(1,128)S(1)}, f32[1,256]{1,0:T(1,128)}, u32[]{:S(2)}) %copy-start) | copy-done | bytes 1048
  1.3 0.0 copy-start.1
  1.3 23.4 %exchange.1 = (bf16[8192,256]{1,0:T(8,128)(2,1)S(1)}, bf16[8192,256]{1,0:T(8,128)(2,1)S(1)}, bf16[8192,256]{1,0:T(8,128)(2,1)S(1)}, bf16[8192,256]{1,0:T(8,128)(...) custom-call(bf16[1,16384,256]{2,1,0:T(8,128)(2,1)} %basis_ref.1, f32[1,256]{1,0:T(1,128)S(1)} %copy-done), custom_call_target="tpu_custom_call" | custom-call | tf_op jit(solution)/shard_map/exchange/pallas_call | solution.py:380
  24.7 0.0 copy-done.1
  24.7 15.2 %subspace.1 = (bf16[512,256]{1,0:T(8,128)(2,1)S(1)}, f32[256,256]{1,0:T(8,128)S(1)}) custom-call(f32[2,16,16,256]{3,2,1,0:T(8,128)S(1)} %get-tuple-element.14.diag_ref, bf16[32,16,128]{2,1,0:T(8,128)(2,1)S(1)} %get-tuple-element.15.cross_ref, f32[512,256]{1,0:T(8,128)S(1)} %copy-done.1), custom_call_target="tpu_custom_call" | custom-call | flops 2147483648 | bytes 83886080 | tf_op jit(solution)/shard_map/subspace/pallas_call | solution.py:414
  40.0 6.3 %fresh.1 = (bf16[1,16384,256]{2,1,0:T(8,128)(2,1)}, f32[1,256,256]{2,1,0:T(8,128)}) custom-call(bf16[8192,256]{1,0:T(8,128)(2,1)S(1)} %get-tuple-element.10.own_a, bf16[8192,256]{1,0:T(8,128)(2,1)S(1)} %get-tuple-element.11.own_b, bf16[8192,256]{1,0:T(8,128)(2,1)S(1)} %get-tuple-element.12.other_a, bf16[8192,256]{1,0:T(8,128)(2,1)S(1)} %get-tuple-element.13.other_b, ...), custom_call_target="tpu_custom_call" | custom-call | tf_op jit(solution)/shard_map/fresh/pallas_call | solution.py:430
Async XLA Ops:
  0.6 0.7 %copy-start = (f32[1,256]{1,0:T(1,128)S(1)}, f32[1,256]{1,0:T(1,128)}, u32[]{:S(2)}) copy-start(f32[1,256]{1,0:T(1,128)} %sing_ref.1) | copy-start | bytes 3076
  1.3 23.4 %copy-start.1 = (f32[512,256]{1,0:T(8,128)S(1)}, f32[512,256]{1,0:T(8,128)}, u32[]{:S(2)}) copy-start(f32[512,256]{1,0:T(8,128)} %sketch_ref.1) | copy-start | bytes 1572868

commit v8 on v7

--- a/solution.py
+++ b/solution.py
@@ -309,8 +309,11 @@
         landed(diag_ref.at[0], sems.at[4])
 
 
-def subspace_kernel(points, diag_ref, cross_ref, sketch_ref, q_ref, corr_ref, high, low):
-    k = corr_ref.shape[0]
+def finish_kernel(
+    points, diag_ref, cross_ref, sketch_ref, own_a, own_b, other_a, other_b, fresh_ref, corr_ref,
+    high, low, q_ref, corr, held, sem, corr_sem,
+):
+    half, k = own_a.shape
     cross = cross_ref[...].astype(jnp.float32).reshape(k // 16, 2, 16, k // 2)
     corner = jnp.concatenate([cross[:, c].reshape(k, k // 2) for c in range(2)], axis=1)
     corner = corner.astype(jnp.bfloat16)
@@ -336,19 +339,7 @@
         block = dot(inverse_factor(dot(y, y, 1, 1)), y, 1, 0)
     q_b = block.T.astype(jnp.bfloat16)
     q_ref[...] = q_b
-    at = lax.rem(lax.axis_index("leaf"), 2)
-    own = pl.ds(pl.multiple_of(at * k, k), k)
-    term = dot(high[own, :], q_b, 1, 0, None) + dot(low[at], q_ref[own, :], 1, 0, None)
-    corr_ref[...] = term * (1.0 / points)
-
-
-def fresh_kernel(
-    own_a, own_b, other_a, other_b, q_ref, corr_in, fresh_ref, corr_ref, held, sem, corr_sem
-):
-    corr_copy = pltpu.make_async_copy(corr_in, corr_ref.at[0], corr_sem)
-    corr_copy.start()
     core = lax.rem(lax.axis_index("leaf"), 2)
-    half, k = own_a.shape
     own = pl.ds(pl.multiple_of(core * k, k), k)
     rest = pl.ds(pl.multiple_of((1 - core) * k, k), k)
     weights = jnp.concatenate([q_ref[own, :], q_ref[rest, :]], axis=0)
@@ -361,11 +352,15 @@
             merged = jnp.concatenate([mine[rows, :], other[rows, :]], axis=1)
             held[at, :] = dot(merged, weights, 1, 0, None).astype(jnp.bfloat16)
             to = fresh_ref.at[0, pl.ds(pl.multiple_of(start + i * TILE, TILE), TILE)]
-            copies.append(pltpu.make_async_copy(held.at[at], to, sem.at[len(copies)]))
+            copies.append(pltpu.make_async_copy(held.at[at], to, sem.at[part * (half // TILE) + i]))
+            copies[-1].start()
+        if part == 0:
+            term = dot(high[own, :], q_b, 1, 0, None) + dot(low[core], q_ref[own, :], 1, 0, None)
+            corr[...] = term * (1.0 / points)
+            copies.append(pltpu.make_async_copy(corr, corr_ref.at[0], corr_sem))
             copies[-1].start()
     for copy in copies:
         copy.wait()
-    corr_copy.wait()
 
 
 def on_device(basis, sing_vals, sketch):
@@ -411,38 +406,26 @@
         ),
         name="exchange",
     )(basis, sing_vals)
-    block_b, correlation = pl.pallas_call(
-        functools.partial(subspace_kernel, points),
-        out_shape=(
-            jax.ShapeDtypeStruct(sketch.shape, jnp.bfloat16),
-            pltpu.VMEM((k, k), f32),
-        ),
-        in_specs=[vmem, vmem, vmem],
-        out_specs=(vmem, vmem),
-        scratch_shapes=[
-            pltpu.VMEM((2 * k, 2 * k), jnp.bfloat16),
-            pltpu.VMEM((2, k, k), jnp.bfloat16),
-        ],
-        compiler_params=pltpu.CompilerParams(vmem_limit_bytes=16 * 2**20),
-        cost_estimate=pl.CostEstimate(flops=2**31, bytes_accessed=80 * 2**20, transcendentals=0),
-        name="subspace",
-    )(diag, cross, sketch)
     return pl.pallas_call(
-        fresh_kernel,
+        functools.partial(finish_kernel, points),
         out_shape=(
             jax.ShapeDtypeStruct((1, rows, k), jnp.bfloat16),
             jax.ShapeDtypeStruct((1, k, k), f32),
         ),
-        in_specs=[vmem] * 6,
+        in_specs=[vmem] * 7,
         out_specs=(any_space, any_space),
         scratch_shapes=[
+            pltpu.VMEM((2 * k, 2 * k), jnp.bfloat16),
+            pltpu.VMEM((2, k, k), jnp.bfloat16),
+            pltpu.VMEM((2 * k, k), jnp.bfloat16),
+            pltpu.VMEM((k, k), f32),
             pltpu.VMEM((rows, k), jnp.bfloat16),
             pltpu.SemaphoreType.DMA((rows // TILE,)),
             pltpu.SemaphoreType.DMA,
         ],
-        compiler_params=pltpu.CompilerParams(vmem_limit_bytes=32 * 2**20),
-        name="fresh",
-    )(own_a, own_b, other_a, other_b, block_b, correlation)
+        compiler_params=pltpu.CompilerParams(vmem_limit_bytes=36 * 2**20),
+        name="finish",
+    )(diag, cross, sketch, own_a, own_b, other_a, other_b)
 
 
 def solution(mesh):

time: 46.6 us -> 46.1 us (0.989)
  Pallas kernels: 44.9 us -> 44.4 us
    pallas_call x2 -> x1, Pallas kernels: 21.5 us -> 21.1 us  [on_device(): pl.pallas_call(functools.partial(finish_kernel, points), out_shape=(jax.S...]
where the time goes in v8:
time: 46.1 us; the launch traced here: 46 us
  Pallas kernels  44.4 us (96%)
  between operations  0.84 us (2%)
  local copies, waits for them, and re-layouts  0.73 us (2%)
    pallas_call x1, Pallas kernels, on_device(): pl.pallas_call(exchange_kernel, out_shape=(pltpu.VMEM((half, k), jnp.bflo...  23.4 us
    pallas_call x1, Pallas kernels, on_device(): pl.pallas_call(functools.partial(finish_kernel, points), out_shape=(jax.S...  21.1 us

profile of v8, /device:TPU:1, one launch (start us, length us, event | category | flops | bytes accessed | tf_op | source)
XLA Modules:
  0.0 46.0 jit_solution(184737547590773392)
XLA Ops:
  0.6 0.0 copy-start
  0.6 0.0 copy-start.1
  0.6 0.7 %copy-done.1 = f32[1,256]{1,0:T(1,128)S(1)} copy-done((f32[1,256]{1,0:T(1,128)S(1)}, f32[1,256]{1,0:T(1,128)}, u32[]{:S(2)}) %copy-start.1) | copy-done | bytes 1048
  1.4 23.4 %exchange.1 = (bf16[8192,256]{1,0:T(8,128)(2,1)S(1)}, bf16[8192,256]{1,0:T(8,128)(2,1)S(1)}, bf16[8192,256]{1,0:T(8,128)(2,1)S(1)}, bf16[8192,256]{1,0:T(8,128)(...) custom-call(bf16[1,16384,256]{2,1,0:T(8,128)(2,1)} %basis_ref.1, f32[1,256]{1,0:T(1,128)S(1)} %copy-done.1), custom_call_target="tpu_custom_call" | custom-call | tf_op jit(solution)/shard_map/exchange/pallas_call | solution.py:375
  24.7 0.0 copy-done
  24.8 21.1 %finish.1 = (bf16[1,16384,256]{2,1,0:T(8,128)(2,1)}, f32[1,256,256]{2,1,0:T(8,128)}) custom-call(f32[2,16,16,256]{3,2,1,0:T(8,128)S(1)} %get-tuple-element.8.diag_ref, bf16[32,16,128]{2,1,0:T(8,128)(2,1)S(1)} %get-tuple-element.9.cross_ref, f32[512,256]{1,0:T(8,128)S(1)} %copy-done, bf16[8192,256]{1,0:T(8,128)(2,1)S(1)} %get-tuple-element.10.own_a, ...), custom_call_target="tpu_custom_call" | custom-call | tf_op jit(solution)/shard_map/finish/pallas_call | solution.py:409
Async XLA Ops:
  0.6 24.1 %copy-start = (f32[512,256]{1,0:T(8,128)S(1)}, f32[512,256]{1,0:T(8,128)}, u32[]{:S(2)}) copy-start(f32[512,256]{1,0:T(8,128)} %sketch_ref.1) | copy-start | bytes 1572868
  0.6 0.7 %copy-start.1 = (f32[1,256]{1,0:T(1,128)S(1)}, f32[1,256]{1,0:T(1,128)}, u32[]{:S(2)}) copy-start(f32[1,256]{1,0:T(1,128)} %sing_ref.1) | copy-start | bytes 3076

commit v9 on v8

--- a/solution.py
+++ b/solution.py
@@ -333,10 +333,11 @@
         rest = dot(lower, high[...], 1, 0, None) + jnp.concatenate(small, axis=1)
         return dot(upper, high[...], 1, 0, None) + rest
 
-    block = sketch_ref[...].T
-    for _ in range(ITERS):
-        y = times_gram(block)
-        block = dot(inverse_factor(dot(y, y, 1, 1)), y, 1, 0)
+    y = times_gram(sketch_ref[...].T)
+    for _ in range(ITERS - 1):
+        ahead = times_gram(y)
+        y = dot(inverse_factor(dot(y, y, 1, 1)), ahead, 1, 0)
+    block = dot(inverse_factor(dot(y, y, 1, 1)), y, 1, 0)
     q_b = block.T.astype(jnp.bfloat16)
     q_ref[...] = q_b
     core = lax.rem(lax.axis_index("leaf"), 2)

time: 46.1 us -> 46 us (level)
  no operation moved by 1% of the time
where the time goes in v9:
time: 46 us; the launch traced here: 45.9 us
  Pallas kernels  44.3 us (96%)
  between operations  0.84 us (2%)
  local copies, waits for them, and re-layouts  0.73 us (2%)
    pallas_call x1, Pallas kernels, on_device(): pl.pallas_call(exchange_kernel, out_shape=(pltpu.VMEM((half, k), jnp.bflo...  23.4 us
    pallas_call x1, Pallas kernels, on_device(): pl.pallas_call(functools.partial(finish_kernel, points), out_shape=(jax.S...  20.9 us

profile of v9, /device:TPU:1, one launch (start us, length us, event | category | flops | bytes accessed | tf_op | source)
XLA Modules:
  0.0 45.9 jit_solution(8898273629026063182)
XLA Ops:
  0.6 0.0 copy-start
  0.6 0.0 copy-start.1
  0.6 0.7 %copy-done.1 = f32[1,256]{1,0:T(1,128)S(1)} copy-done((f32[1,256]{1,0:T(1,128)S(1)}, f32[1,256]{1,0:T(1,128)}, u32[]{:S(2)}) %copy-start.1) | copy-done | bytes 1048
  1.4 23.4 %exchange.1 = (bf16[8192,256]{1,0:T(8,128)(2,1)S(1)}, bf16[8192,256]{1,0:T(8,128)(2,1)S(1)}, bf16[8192,256]{1,0:T(8,128)(2,1)S(1)}, bf16[8192,256]{1,0:T(8,128)(...) custom-call(bf16[1,16384,256]{2,1,0:T(8,128)(2,1)} %basis_ref.1, f32[1,256]{1,0:T(1,128)S(1)} %copy-done.1), custom_call_target="tpu_custom_call" | custom-call | tf_op jit(solution)/shard_map/exchange/pallas_call | solution.py:376
  24.7 0.0 copy-done
  24.8 20.9 %finish.1 = (bf16[1,16384,256]{2,1,0:T(8,128)(2,1)}, f32[1,256,256]{2,1,0:T(8,128)}) custom-call(f32[2,16,16,256]{3,2,1,0:T(8,128)S(1)} %get-tuple-element.8.diag_ref, bf16[32,16,128]{2,1,0:T(8,128)(2,1)S(1)} %get-tuple-element.9.cross_ref, f32[512,256]{1,0:T(8,128)S(1)} %copy-done, bf16[8192,256]{1,0:T(8,128)(2,1)S(1)} %get-tuple-element.10.own_a, ...), custom_call_target="tpu_custom_call" | custom-call | tf_op jit(solution)/shard_map/finish/pallas_call | solution.py:410
Async XLA Ops:
  0.6 24.1 %copy-start = (f32[512,256]{1,0:T(8,128)S(1)}, f32[512,256]{1,0:T(8,128)}, u32[]{:S(2)}) copy-start(f32[512,256]{1,0:T(8,128)} %sketch_ref.1) | copy-start | bytes 1572868
  0.6 0.7 %copy-start.1 = (f32[1,256]{1,0:T(1,128)S(1)}, f32[1,256]{1,0:T(1,128)}, u32[]{:S(2)}) copy-start(f32[1,256]{1,0:T(1,128)} %sing_ref.1) | copy-start | bytes 3076
